TPU v7x, 128 devices: a whole 4x4x4 slice. The times are simulated.
128 devices in a mesh: row: 16 (over z, y), col: 8 (over x, core).
Axes of the slice: x: 4, y: 4, z: 4, core: 2. Of those that a mesh axis runs over, the one named last changes fastest.
Arguments:
- tractions: float32 [3, 512, 32768], P(None, None, ('row', 'col')), may hold values from -1 to 1
- log_state: float32 [512, 32768], P(None, ('row', 'col')), may hold values from -0.5 to 1
- rate_coef: float32 [32768], P(('row', 'col')), may hold values from 0.8 to 1.6
- state_coef: float32 [32768], P(('row', 'col')), may hold values from 0.2 to 0.8
- normal_stress: float32 [32768], P(('row', 'col')), may hold values from 0.5 to 4
- inv_length: float32 [32768], P(('row', 'col')), may hold values from 0.5 to 2
- near_blocks: bfloat16 [128, 3, 3, 2, 256, 256], P(('row', 'col'))
- far_right: bfloat16 [128, 128, 2, 32, 256], P('row', 'col'), may hold values from -0.25 to 0.25
- far_left: bfloat16 [128, 128, 3, 32, 256], P(('row', 'col')), may hold values from -0.25 to 0.25
- ranks: int32 [128, 128], P('row', 'col'), may hold values from 13 to 32, as said below
Outputs:
- new_tractions: float32 [3, 512, 32768], P(None, None, ('row', 'col'))
- new_state: float32 [512, 32768], P(None, ('row', 'col'))
Inputs may be any that keep to these rules, and one draw needn't show every extreme that they name: ranks[a, b] rank slots of lattice block (a, b) are used.
All inputs are finite; a program needn't handle non-finite values.
Results may differ from a plain program's by a relative error of at most 0.0003.
Values may be sent and summed in bfloat16 or wider, within the bound.
No kernel may reach another device: no remote copies, remote signals or barrier semaphores. Data moves between devices by JAX's collectives and lax.ppermute only.
A program may use at most 128 MiB of HBM per device.

v0:
```python
import jax
import jax.numpy as jnp
from jax import lax
from jax.sharding import PartitionSpec as P

time_step = 0.03


def padded_2(cells, sides, width):
    for axis, dim in sides:
        count = lax.axis_size(axis)
        ends = count - 1
        head = lax.slice_in_dim(cells, 0, width, axis=dim)
        tail = lax.slice_in_dim(cells, cells.shape[dim] - width, cells.shape[dim], axis=dim)
        cells = jnp.concatenate(
            [
                lax.ppermute(tail, axis, [(i, (i + 1) % count) for i in range(ends)]),
                cells,
                lax.ppermute(head, axis, [((i + 1) % count, i) for i in range(ends)]),
            ],
            axis=dim,
        )
    return cells


def friction_slip(traction, log_value, rate_coef, state_coef, normal_stress):
    effective = jnp.maximum(normal_stress - traction[2], 1.0)
    scaled = rate_coef * effective
    shear_size = jnp.sqrt(traction[0] * traction[0] + traction[1] * traction[1])
    stress_ratio = shear_size / scaled
    amplitude = 2.0 * jnp.exp(-state_coef * log_value / rate_coef) * jnp.sinh(stress_ratio)
    factor = amplitude / (scaled * jnp.maximum(stress_ratio, 1.0))
    slip_rates = jnp.stack([factor * traction[0], factor * traction[1]]).astype(jnp.bfloat16)
    slip_speed = amplitude * jnp.minimum(stress_ratio, 1.0)
    return (slip_rates, slip_speed)


def masked_coefficients(weights, slip_rates, active, pattern):
    values = jnp.einsum(pattern, weights, slip_rates, preferred_element_type=jnp.float32)
    return jnp.where(active[..., None], values, 0.0).astype(jnp.bfloat16)


def on_device(
    tractions,
    log_state,
    rate_coef,
    state_coef,
    normal_stress,
    inv_length,
    near_blocks,
    far_right,
    far_left,
    ranks,
):
    col_count = lax.axis_size("col")
    row_index = lax.axis_index("row")
    col_index = lax.axis_index("col")
    tile_rows = far_right.shape[0]
    tile_cols = far_right.shape[1]
    rank_width = far_right.shape[3]
    rank_slots = jnp.arange(rank_width, dtype=jnp.int32)
    row_blocks = row_index * tile_rows + jnp.arange(tile_rows, dtype=jnp.int32)
    column_block = jnp.arange(tile_cols, dtype=jnp.int32) * col_count + col_index
    distance = jnp.abs(row_blocks[:, None] - column_block[None, :])
    active = (rank_slots[None, None, :] < ranks[:, :, None]) & (distance >= 2)[:, :, None]

    def fault_rates(traction_now, state_now):
        slip_rates, slip_speed = friction_slip(
            traction_now, state_now, rate_coef, state_coef, normal_stress
        )
        members = slip_rates.shape[1]
        cells = slip_rates.shape[2]
        padded = padded_2(slip_rates, ((("row", "col"), 2),), cells)
        beside_all = padded.reshape(2, members, 3, cells)
        near_rates = jnp.einsum(
            "kcspq,sekq->cep", near_blocks[0], beside_all, preferred_element_type=jnp.float32
        )
        gathered = lax.all_gather(slip_rates, "row", axis=2, tiled=True)
        blocks = gathered.reshape(2, members, tile_cols, cells)
        coefficients = masked_coefficients(far_right, blocks, active, "absrp,sebp->abre")
        arrived = lax.all_to_all(coefficients, "col", split_axis=0, concat_axis=1, tiled=True)
        far_rates = jnp.einsum(
            "bre,bkrp->kep", arrived[0], far_left[0], preferred_element_type=jnp.float32
        )
        state_rates = (jnp.exp(-state_now) - slip_speed) * inv_length
        return (near_rates + far_rates, state_rates)

    first_rates, first_state = fault_rates(tractions, log_state)
    middle = tractions + time_step * first_rates
    middle_state = log_state + time_step * first_state
    second_rates, second_state = fault_rates(middle, middle_state)
    new_tractions = tractions + 0.5 * time_step * (first_rates + second_rates)
    new_state = log_state + 0.5 * time_step * (first_state + second_state)
    return (new_tractions, new_state)


def solution(mesh):
    placed = (
        P(None, None, ("row", "col")),
        P(None, ("row", "col")),
        P(("row", "col")),
        P(("row", "col")),
        P(("row", "col")),
        P(("row", "col")),
        P(("row", "col"), None, None, None, None, None),
        P("row", "col", None, None, None),
        P(("row", "col"), None, None, None, None),
        P("row", "col"),
    )
    return jax.shard_map(
        on_device,
        mesh=mesh,
        in_specs=placed,
        out_specs=(P(None, None, ("row", "col")), P(None, ("row", "col"))),
        check_vma=False,
    )
```

profile of v0, /device:TPU:32, one launch (start us, length us, event | category | flops | bytes accessed | tf_op | source)
XLA Modules:
  0.0 333.8 jit_solution(15866650213489543570)
XLA Ops:
  9.3 3.0 copy.85
  12.4 2.8 fusion.44
  17.5 72.6 %all-gather.3.cloned.1.call-done = bf16[2,512,4096]{1,2,0:T(8,128)(2,1)} async-done(((bf16[2,512,256]{1,2,0:T(8,128)(2,1)}), bf16[2,512,4096]{1,2,0:T(8,128)(2,1)}) %all-gather.3.cloned.1.call-update) | async-done | bytes 8388624 | tf_op jit(solution)/shard_map/all_gather | solution.py:78
  90.1 6.0 %fusion.1 = bf16[8,16,32,512]{3,2,0,1:T(8,128)(2,1)S(1)} fusion(pred[8,16,32]{2,0,1:T(8,128)(4,1)S(1)} %fusion.48, bf16[8,16,2,32,256]{4,3,2,1,0:T(8,128)(2,1)} %param.17, bf16[2,512,16,256,1]{1,3,2,0,4:T(8,128)(2,1)} %bitcast.170), kind=kOutput, calls=%fused_computation.3 | convolution fusion | flops 2151677952 | bytes 16781312 | tf_op jit(solution)/shard_map/absrp,sebp->abre/dot_general | solution.py:39
  96.0 2.4 copy.72
  98.4 4.6 %all-to-all-start = ((bf16[8,16,32,512]{3,2,1,0:T(8,128)(2,1)}), bf16[8,16,32,512]{3,2,1,0:T(8,128)(2,1)}, u32[]{:S(2)}, u32[]{:S(2)}) async-start(bf16[8,16,32,512]{3,2,1,0:T(8,128)(2,1)} %copy.72), calls=%async_computation | async-start | bytes 8388608 | tf_op jit(solution)/shard_map/all_to_all | solution.py:81
  103.0 7.0 %collective-permute-start.1 = (bf16[2,512,256]{1,2,0:T(8,128)(2,1)}, bf16[2,512,256]{1,2,0:T(8,128)(2,1)S(1)}, u32[]{:S(2)}, u32[]{:S(2)}) collective-permute-start(bf16[2,512,256]{1,2,0:T(8,128)(2,1)} %pad_maximum_fusion.2), channel_id=1, source_target_pairs={{1,0},{2,1},{3,2},{4,3},{5,4},{6,5},{7,6},{8,7},{9,8},{10,9},{11,1... | collective-permute-start | bytes 1572872 | tf_op jit(solution)/shard_map/ppermute | solution.py:19
  112.0 42.6 %collective-permute-done.1 = bf16[2,512,256]{1,2,0:T(8,128)(2,1)S(1)} collective-permute-done((bf16[2,512,256]{1,2,0:T(8,128)(2,1)}, bf16[2,512,256]{1,2,0:T(8,128)(2,1)S(1)}, u32[]{:S(2)}, u32[]{:S(2)}) %collective-permute-start.1) | collective-permute-done | bytes 524320 | tf_op jit(solution)/shard_map/ppermute | solution.py:19
  154.6 5.6 %collective-permute-done = bf16[2,512,256]{1,2,0:T(8,128)(2,1)S(1)} collective-permute-done((bf16[2,512,256]{1,2,0:T(8,128)(2,1)}, bf16[2,512,256]{1,2,0:T(8,128)(2,1)S(1)}, u32[]{:S(2)}, u32[]{:S(2)}) %collective-permute-start) | collective-permute-done | bytes 524320 | tf_op jit(solution)/shard_map/ppermute | solution.py:17
  161.5 7.0 %fusion.6 = f32[512,3,256,1]{0,2,1,3:T(8,128)S(1)} fusion(bf16[128,32,512,1]{2,1,3,0:T(8,128)(2,1)} %bitcast.51, bf16[1,128,3,32,256]{4,3,2,1,0:T(8,128)(2,1)} %param.18), kind=kOutput, calls=%fused_computation.8 | convolution fusion | flops 3221225472 | bytes 12058624 | tf_op jit(solution)/shard_map/bre,bkrp->kep/dot_general | solution.py:82
  168.5 2.6 bitcast_add_fusion.2
  171.1 2.5 fusion.46
  174.6 67.0 %all-gather.5.cloned.1.call-done = bf16[2,512,4096]{1,2,0:T(8,128)(2,1)} async-done(((bf16[2,512,256]{1,2,0:T(8,128)(2,1)}), bf16[2,512,4096]{1,2,0:T(8,128)(2,1)}) %all-gather.5.cloned.1.call-update) | async-done | bytes 8388624 | tf_op jit(solution)/shard_map/all_gather | solution.py:78
  241.6 6.0 %fusion = bf16[8,16,32,512]{3,2,0,1:T(8,128)(2,1)S(1)} fusion(pred[8,16,32]{2,0,1:T(8,128)(4,1)S(1)} %fusion.48, bf16[8,16,2,32,256]{4,3,2,1,0:T(8,128)(2,1)} %param.17, bf16[2,512,16,256,1]{1,3,2,0,4:T(8,128)(2,1)} %bitcast.171), kind=kOutput, calls=%fused_computation.1 | convolution fusion | flops 2151677952 | bytes 16781312 | tf_op jit(solution)/shard_map/absrp,sebp->abre/dot_general | solution.py:39
  247.5 2.4 copy.81
  249.9 4.6 %all-to-all-start.1 = ((bf16[8,16,32,512]{3,2,1,0:T(8,128)(2,1)}), bf16[8,16,32,512]{3,2,1,0:T(8,128)(2,1)}, u32[]{:S(2)}, u32[]{:S(2)}) async-start(bf16[8,16,32,512]{3,2,1,0:T(8,128)(2,1)} %copy.81), calls=%async_computation.1 | async-start | bytes 8388608 | tf_op jit(solution)/shard_map/all_to_all | solution.py:81
  254.5 7.1 %collective-permute-start.3 = (bf16[2,512,256]{1,2,0:T(8,128)(2,1)}, bf16[2,512,256]{1,2,0:T(8,128)(2,1)}, u32[]{:S(2)}, u32[]{:S(2)}) collective-permute-start(bf16[2,512,256]{1,2,0:T(8,128)(2,1)} %pad_maximum_fusion.3), channel_id=1, source_target_pairs={{1,0},{2,1},{3,2},{4,3},{5,4},{6,5},{7,6},{8,7},{9,8},{10,9},{11,1... | collective-permute-start | bytes 1572872 | tf_op jit(solution)/shard_map/ppermute | solution.py:19
  261.6 2.1 collective-permute-start.2
  265.7 40.4 %collective-permute-done.3 = bf16[2,512,256]{1,2,0:T(8,128)(2,1)} collective-permute-done((bf16[2,512,256]{1,2,0:T(8,128)(2,1)}, bf16[2,512,256]{1,2,0:T(8,128)(2,1)}, u32[]{:S(2)}, u32[]{:S(2)}) %collective-permute-start.3) | collective-permute-done | bytes 524320 | tf_op jit(solution)/shard_map/ppermute | solution.py:19
  306.1 5.7 %collective-permute-done.2 = bf16[2,512,256]{1,2,0:T(8,128)(2,1)} collective-permute-done((bf16[2,512,256]{1,2,0:T(8,128)(2,1)}, bf16[2,512,256]{1,2,0:T(8,128)(2,1)}, u32[]{:S(2)}, u32[]{:S(2)}) %collective-permute-start.2) | collective-permute-done | bytes 524320 | tf_op jit(solution)/shard_map/ppermute | solution.py:17
  311.8 2.5 pad_maximum_fusion.1
  314.3 7.0 %fusion.8 = f32[512,3,256,1]{0,2,1,3:T(8,128)S(1)} fusion(bf16[128,32,512,1]{2,1,3,0:T(8,128)(2,1)} %bitcast.53, bf16[1,128,3,32,256]{4,3,2,1,0:T(8,128)(2,1)} %param.18), kind=kOutput, calls=%fused_computation.10 | convolution fusion | flops 3221225472 | bytes 12058624 | tf_op jit(solution)/shard_map/bre,bkrp->kep/dot_general | solution.py:82
  321.3 2.6 fusion.27
  323.9 3.0 copy.87
  (42 shorter events, 10.7 us)
Async XLA Ops:
  7.2 161.3 %copy-start = (bf16[1,3,3,2,256,256]{5,4,3,2,1,0:T(8,128)(2,1)S(1)}, bf16[1,3,3,2,256,256]{5,4,3,2,1,0:T(8,128)(2,1)}, u32[]{:S(2)}) copy-start(bf16[1,3,3,2,256,256]{5,4,3,2,1,0:T(8,128)(2,1)} %param.16) | copy-start | bytes 7077892
  7.2 5.2 %copy-start.7 = (f32[256]{0:T(256)S(1)}, f32[256]{0:T(256)}, u32[]{:S(2)}) copy-start(f32[256]{0:T(256)} %param.14) | copy-start | bytes 3076
  7.2 5.2 %copy-start.8 = (f32[256]{0:T(256)S(1)}, f32[256]{0:T(256)}, u32[]{:S(2)}) copy-start(f32[256]{0:T(256)} %param.12) | copy-start | bytes 3076
  7.2 82.9 %all-gather.3.cloned.1.call-start = ((), (), s32[]{:S(2)}) async-start(), calls=%async_computation.2 | async-start | bytes 8912896 | tf_op jit(solution)/shard_map/all_gather | solution.py:78
  12.4 4.9 %copy-start.9 = (s32[8,16]{1,0:T(8,128)S(1)}, s32[8,16]{1,0:T(8,128)}, u32[]{:S(2)}) copy-start(s32[8,16]{1,0:T(8,128)} %param.19) | copy-start | bytes 1540
  98.4 63.1 %all-to-all-start = ((bf16[8,16,32,512]{3,2,1,0:T(8,128)(2,1)}), bf16[8,16,32,512]{3,2,1,0:T(8,128)(2,1)}, u32[]{:S(2)}, u32[]{:S(2)}) async-start(bf16[8,16,32,512]{3,2,1,0:T(8,128)(2,1)} %copy.72), calls=%async_computation | async-start | bytes 8388608 | tf_op jit(solution)/shard_map/all_to_all | solution.py:81
  102.9 138.6 %all-gather.5.cloned.1.call-start = ((), (), s32[]{:S(2)}) async-start(), calls=%async_computation.3 | async-start | bytes 8912896 | tf_op jit(solution)/shard_map/all_gather | solution.py:78
  103.0 51.6 %collective-permute-start.1 = (bf16[2,512,256]{1,2,0:T(8,128)(2,1)}, bf16[2,512,256]{1,2,0:T(8,128)(2,1)S(1)}, u32[]{:S(2)}, u32[]{:S(2)}) collective-permute-start(bf16[2,512,256]{1,2,0:T(8,128)(2,1)} %pad_maximum_fusion.2), channel_id=1, source_target_pairs={{1,0},{2,1},{3,2},{4,3},{5,4},{6,5},{7,6},{8,7},{9,8},{10,9},{11,1... | collective-permute-start | bytes 1572872 | tf_op jit(solution)/shard_map/ppermute | solution.py:19
  110.0 50.1 %collective-permute-start = (bf16[2,512,256]{1,2,0:T(8,128)(2,1)}, bf16[2,512,256]{1,2,0:T(8,128)(2,1)S(1)}, u32[]{:S(2)}, u32[]{:S(2)}) collective-permute-start(bf16[2,512,256]{1,2,0:T(8,128)(2,1)} %pad_maximum_fusion.2), channel_id=1, source_target_pairs={{0,1},{1,2},{2,3},{3,4},{4,5},{5,6},{6,7},{7,8},{8,9},{9,10},{10,1... | collective-permute-start | bytes 1572872 | tf_op jit(solution)/shard_map/ppermute | solution.py:17
  161.4 7.0 %copy-start.1 = (f32[3,512,256]{1,2,0:T(8,128)S(1)}, f32[3,512,256]{1,2,0:T(8,128)}, u32[]{:S(2)}) copy-start(f32[3,512,256]{1,2,0:T(8,128)} %copy.85) | copy-start | bytes 4718596
  161.4 7.0 %copy-start.3 = (bf16[2,512,768]{1,2,0:T(8,128)(2,1)S(1)}, bf16[2,512,768]{1,2,0:T(8,128)(2,1)}, u32[]{:S(2)}) copy-start(bf16[2,512,768]{1,2,0:T(8,128)(2,1)} %pad_maximum_fusion) | copy-start | bytes 4718596
  168.5 2.7 copy-start.4
  168.5 2.6 copy-start.10
  249.9 64.3 %all-to-all-start.1 = ((bf16[8,16,32,512]{3,2,1,0:T(8,128)(2,1)}), bf16[8,16,32,512]{3,2,1,0:T(8,128)(2,1)}, u32[]{:S(2)}, u32[]{:S(2)}) async-start(bf16[8,16,32,512]{3,2,1,0:T(8,128)(2,1)} %copy.81), calls=%async_computation.1 | async-start | bytes 8388608 | tf_op jit(solution)/shard_map/all_to_all | solution.py:81
  254.5 51.6 %collective-permute-start.3 = (bf16[2,512,256]{1,2,0:T(8,128)(2,1)}, bf16[2,512,256]{1,2,0:T(8,128)(2,1)}, u32[]{:S(2)}, u32[]{:S(2)}) collective-permute-start(bf16[2,512,256]{1,2,0:T(8,128)(2,1)} %pad_maximum_fusion.3), channel_id=1, source_target_pairs={{1,0},{2,1},{3,2},{4,3},{5,4},{6,5},{7,6},{8,7},{9,8},{10,9},{11,1... | collective-permute-start | bytes 1572872 | tf_op jit(solution)/shard_map/ppermute | solution.py:19
  261.6 50.2 %collective-permute-start.2 = (bf16[2,512,256]{1,2,0:T(8,128)(2,1)}, bf16[2,512,256]{1,2,0:T(8,128)(2,1)}, u32[]{:S(2)}, u32[]{:S(2)}) collective-permute-start(bf16[2,512,256]{1,2,0:T(8,128)(2,1)} %pad_maximum_fusion.3), channel_id=1, source_target_pairs={{0,1},{1,2},{2,3},{3,4},{4,5},{5,6},{6,7},{7,8},{8,9},{9,10},{10,1... | collective-permute-start | bytes 1572872 | tf_op jit(solution)/shard_map/ppermute | solution.py:17
  314.2 7.0 %copy-start.2 = (f32[3,512,256]{1,2,0:T(8,128)S(1)}, f32[3,512,256]{1,2,0:T(8,128)}, u32[]{:S(2)}) copy-start(f32[3,512,256]{1,2,0:T(8,128)} %copy.85) | copy-start | bytes 4718596
  314.2 7.0 %copy-start.5 = (f32[512,3,256]{0,2,1:T(8,128)S(1)}, f32[512,3,256]{0,2,1:T(8,128)}, u32[]{:S(2)}) copy-start(f32[512,3,256]{0,2,1:T(8,128)} %get-tuple-element.15) | copy-start | bytes 4718596
  314.2 7.0 %copy-start.6 = (bf16[2,512,768]{1,2,0:T(8,128)(2,1)S(1)}, bf16[2,512,768]{1,2,0:T(8,128)(2,1)}, u32[]{:S(2)}) copy-start(bf16[2,512,768]{1,2,0:T(8,128)(2,1)} %pad_maximum_fusion.1) | copy-start | bytes 4718596
Sparse Core Ops, SparseCore 0:
  17.3 72.6 all-gather.2
  174.7 66.7 all-gather.4
where the time goes:
time: 334 us
  waiting for transfers between devices  234 us (70%)
  matrix products  31.1 us (9%)
  starting transfers between devices  27.4 us (8%)
  between operations  14.3 us (4%)
  local copies, waits for them, and re-layouts  14.2 us (4%)
  other arithmetic  13.1 us (4%)
    all_gather x2, waiting for transfers between devices, fault_rates(): gathered = lax.all_gather(slip_rates, 'row', axis=2, tiled=True)  140 us
    ppermute x2, waiting for transfers between devices, padded_2(): lax.ppermute(head, axis, [((i + 1) % count, i) for i in range(ends)])  83 us
    ppermute x2, starting transfers between devices, padded_2(): lax.ppermute(head, axis, [((i + 1) % count, i) for i in range(ends)])  14.1 us
    dot_general x2, matrix products, fault_rates(): jnp.einsum('bre,bkrp->kep', arrived[0], far_left[0], preferred_element_ty...  14 us
    dot_general x2, matrix products, masked_coefficients(): jnp.einsum(pattern, weights, slip_rates, preferred_element_type=jnp.float32)  11.9 us
    ppermute x2, waiting for transfers between devices, padded_2(): lax.ppermute(tail, axis, [(i, (i + 1) % count) for i in range(ends)])  11.2 us
    unnamed x27, local copies, waits for them, and re-layouts  9.44 us
    all_to_all x2, starting transfers between devices, fault_rates(): lax.all_to_all(coefficients, 'col', split_axis=0, concat_axis=1, tiled=True)  9.13 us
  transfers between devices with their start and end apart: 8, of which 6 were waited for; matrix products, arithmetic and copies ran while one was open for 2% of the time, Pallas kernels for 0%

commit v1 on v0

v1 whole, which is shorter than its diff:
```python
import functools
import math

import jax
import jax.numpy as jnp
from jax import lax
from jax.experimental import pallas as pl
from jax.experimental.pallas import tpu as pltpu
from jax.sharding import Mesh
from jax.sharding import PartitionSpec as P

time_step = 0.03
PARTS = 2
SIDE = 4
CORES = 2
OFFSETS = (0, 1, 3, 2)
ALL = ("z", "y", "x", "core")
VMEM = 60 * 2**20
ANY = pl.BlockSpec(memory_space=pl.ANY)
NT = (((1,), (1,)), ((), ()))


def sinh(x):
    small = x * x
    series = x * (1.0 + small * (1.0 / 6 + small * (1.0 / 120 + small * (1.0 / 5040))))
    exact = jnp.exp(x - math.log(2.0)) - jnp.exp(-x - math.log(2.0))
    return jnp.where(x < 0.35, series, exact)


def friction_slip(traction, log_value, rate_coef, state_coef, normal_stress):
    effective = jnp.maximum(normal_stress - traction[2], 1.0)
    scaled = rate_coef * effective
    shear_size = jnp.sqrt(traction[0] * traction[0] + traction[1] * traction[1])
    stress_ratio = shear_size / scaled
    amplitude = 2.0 * jnp.exp(-state_coef * log_value / rate_coef) * sinh(stress_ratio)
    factor = amplitude / (scaled * jnp.maximum(stress_ratio, 1.0))
    slip_rates = [(factor * traction[s]).astype(jnp.bfloat16) for s in range(2)]
    slip_speed = amplitude * jnp.minimum(stress_ratio, 1.0)
    return (slip_rates, slip_speed)


def beside(slabs, step):
    count = SIDE**3 * CORES
    pairs = [(i, i - step) for i in range(count) if 0 <= i - step < count]
    return lax.ppermute(slabs, ALL, pairs)


def from_z(slabs, dz):
    return lax.ppermute(slabs, "z", [((i + dz) % SIDE, i) for i in range(SIDE)])


def whole(v):
    return pl.BlockSpec(v.shape, lambda *_: (0,) * len(v.shape))


def call(kernel, name, grid, in_specs, out_specs, out_shape, args, flops, scratch=(), aliases=None):
    return pl.pallas_call(
        kernel,
        grid=grid,
        in_specs=in_specs,
        out_specs=out_specs,
        out_shape=out_shape,
        scratch_shapes=list(scratch),
        input_output_aliases=aliases or {},
        compiler_params=pltpu.CompilerParams(vmem_limit_bytes=VMEM),
        cost_estimate=pl.CostEstimate(flops=flops, bytes_accessed=8 * 2**20, transcendentals=0),
        name=name,
    )(*args)


def mask_kernel(used, right, out):
    rows, _, columns, _, width, _ = right.shape
    zb = pl.program_id(0)
    slot = lax.broadcasted_iota(jnp.int32, right.shape[4:], 0)
    for yb in range(columns):
        for a in range(rows):
            active = slot < used[a, zb * columns + yb]
            for s in range(2):
                value = right[a, 0, yb, s]
                out[yb, 0, s, a] = jnp.where(active, value, jnp.zeros_like(value))


def masked_right(far_right, used):
    rows, _, _, width, cells = far_right.shape
    right = far_right.reshape(rows, SIDE, SIDE, 2, width, cells)
    return call(
        mask_kernel,
        "mask",
        (SIDE,),
        [
            pl.BlockSpec(memory_space=pltpu.SMEM),
            pl.BlockSpec((rows, 1, SIDE, 2, width, cells), lambda z: (0, z, 0, 0, 0, 0)),
        ],
        pl.BlockSpec((SIDE, 1, 2, rows, width, cells), lambda z: (0, z, 0, 0, 0, 0)),
        jax.ShapeDtypeStruct((SIDE, SIDE, 2, rows, width, cells), far_right.dtype),
        (used, right),
        0,
    )


def turn_kernel(left, out):
    cols, planes, _, sides, width, cells = left.shape
    row = lax.broadcasted_iota(jnp.int32, (cells, cells), 0)
    column = lax.broadcasted_iota(jnp.int32, (cells, cells), 1)
    unit = jnp.where(row == column, 1.0, 0.0).astype(left.dtype)
    for c in range(sides):
        block = jnp.concatenate([left[i, j, 0, c] for i in range(cols) for j in range(planes)], axis=0)
        turned = lax.dot_general(unit, block, NT, preferred_element_type=jnp.float32)
        out[c * cells : (c + 1) * cells] = turned.astype(out.dtype)


def turned_left(far_left):
    count, sides, width, cells = far_left.shape
    cols = count // SIDE**2
    left = far_left.reshape(cols, SIDE, SIDE, sides, width, cells)
    pair = cells // (SIDE * width)
    return call(
        turn_kernel,
        "turn",
        (SIDE, cols // pair),
        [pl.BlockSpec((pair, SIDE, 1, sides, width, cells), lambda y, j: (j, 0, y, 0, 0, 0))],
        pl.BlockSpec((sides * cells, cells), lambda y, j: (0, y * (cols // pair) + j)),
        jax.ShapeDtypeStruct((sides * cells, count * width), far_left.dtype),
        (left,),
        0,
    )


def coefficient_kernel(planes, *refs):
    slips, weights, out = refs[: len(OFFSETS)], refs[len(OFFSETS)], refs[-1]
    _, _, _, rows, width, cells = weights.shape
    for i, slip in enumerate(slips):
        z = planes[i]
        parts = [weights[0, z, s].reshape(rows * width, cells) for s in range(2)]
        value = jnp.dot(
            jnp.concatenate(parts, axis=1), slip[...], preferred_element_type=jnp.float32
        )
        out[:, z] = value.astype(jnp.bfloat16).reshape(rows, width, value.shape[1])


def coefficients_of(around, planes, weights, after=()):
    depth, members = around[0].shape
    lines, count, _, rows, width, cells = weights.shape
    return call(
        coefficient_kernel,
        "coefficients",
        (lines,),
        [pl.BlockSpec(memory_space=pltpu.SMEM)]
        + [whole(v) for v in around]
        + [pl.BlockSpec((1, count, 2, rows, width, cells), lambda y: (y, 0, 0, 0, 0, 0))]
        + [ANY] * len(after),
        pl.BlockSpec((rows, count, width, members), lambda y: (y, 0, 0, 0)),
        jax.ShapeDtypeStruct((lines * rows, count, width, members), jnp.bfloat16),
        (planes, *around, weights, *after),
        2 * lines * count * rows * width * depth * members,
    )


def add_far(coef, weights, near, total):
    part = jnp.dot(weights[...], coef[...], preferred_element_type=jnp.float32)
    step = pl.program_id(0)

    @pl.when(step == 0)
    def _():
        total[...] = near[...] + part

    @pl.when(step > 0)
    def _():
        total[...] += part

    return step == pl.num_programs(0) - 1


def first_kernel(
    coef, weights, near, tractions, middle_state, half_state, columns, *refs,
):
    slips, half_tractions, new_state, total = refs[-4:]
    sides, cells, _ = tractions.shape

    @pl.when(add_far(coef, weights, near, total))
    def _():
        middle = []
        for c in range(sides):
            rates = total[c * cells : (c + 1) * cells]
            old = tractions[c]
            middle.append(old + time_step * rates)
            half_tractions[c] = old + 0.5 * time_step * rates
        state = middle_state[...]
        slip_rates, speed = friction_slip(
            middle, state, *[columns[:, k : k + 1] for k in range(3)]
        )
        for s in range(2):
            slips[s * cells : (s + 1) * cells] = slip_rates[s]
        state_rates = (jnp.exp(-state) - speed) * columns[:, 3:]
        new_state[...] = half_state[...] + 0.5 * time_step * state_rates


def second_kernel(coef, weights, near, half_tractions, *refs):
    new_tractions, total = refs[-2:]
    sides, cells, _ = half_tractions.shape

    @pl.when(add_far(coef, weights, near, total))
    def _():
        for c in range(sides):
            rates = total[c * cells : (c + 1) * cells]
            new_tractions[c] = (half_tractions[c] + 0.5 * time_step * rates).T


def far_specs(coef, weights, steps):
    depth, members = coef.shape
    return [
        pl.BlockSpec((depth // steps, members), lambda k: (k, 0)),
        pl.BlockSpec((weights.shape[0], depth // steps), lambda k: (0, k)),
    ]


def near_kernel(x0, x1, x2, weights, out):
    cells = weights.shape[3]
    total = None
    for k, x in enumerate((x0, x1, x2)):
        part = jnp.dot(
            jnp.concatenate([weights[k, 0, s] for s in range(2)], axis=1),
            x[...],
            preferred_element_type=jnp.float32,
        )
        total = part if total is None else total + part
    out[...] = total


def near_part(slabs, near_blocks):
    depth, members = slabs[0].shape
    sides, cells = near_blocks.shape[1], near_blocks.shape[3]
    return call(
        near_kernel,
        "near",
        (sides,),
        [whole(slabs[0])] * 3 + [pl.BlockSpec((3, 1, 2, cells, cells), lambda c: (0, c, 0, 0, 0))],
        pl.BlockSpec((cells, members), lambda c: (c, 0)),
        jax.ShapeDtypeStruct((sides * cells, members), jnp.float32),
        (*slabs, near_blocks),
        2 * 3 * sides * cells * depth * members,
    )


def on_device(
    tractions, log_state, rate_coef, state_coef, normal_stress, inv_length,
    near_blocks, far_right, far_left, ranks,
):
    place = {axis: lax.axis_index(axis) for axis in ALL}
    row = place["z"] * SIDE + place["y"]
    col = place["x"] * CORES + place["core"]
    tile_rows, tile_cols, _, width, cells = far_right.shape
    all_members = log_state.shape[0]
    members = all_members // PARTS
    sides = far_left.shape[2]

    block_row = row * tile_rows + jnp.arange(tile_rows, dtype=jnp.int32)
    block_col = jnp.arange(tile_cols, dtype=jnp.int32) * tile_rows + col
    near = jnp.abs(block_row[:, None] - block_col[None, :]) < 2
    right = masked_right(far_right, jnp.where(near, 0, ranks))
    right = lax.all_to_all(right, "y", split_axis=0, concat_axis=0, tiled=True)
    left = turned_left(far_left[0])
    columns = jnp.stack([rate_coef, state_coef, normal_stress, inv_length], axis=1)

    planes = jnp.stack([(place["z"] + dz) % SIDE for dz in OFFSETS])

    def gathered(slips):
        return [slips] + [from_z(slips, dz) for dz in OFFSETS[1:]]

    def sent(coef):
        coef = coef.reshape(coef.shape[0], -1, members)
        coef = lax.all_to_all(coef, ("y", "x", "core"), split_axis=0, concat_axis=0, tiled=True)
        return coef.reshape(-1, members)

    steps = 4
    flops = 2 * sides * cells * left.shape[1] * members
    scratch = [pltpu.VMEM((sides * cells, members), jnp.float32)]

    def start(part):
        here = slice(part * members, (part + 1) * members)
        old = jnp.swapaxes(tractions[:, here], 1, 2)
        state = jnp.swapaxes(log_state[here], 0, 1)
        slip_rates, speed = friction_slip(old, state, *[columns[:, k : k + 1] for k in range(3)])
        slips = jnp.concatenate(slip_rates, axis=0)
        state_rates = (jnp.exp(-state) - speed) * columns[:, 3:]
        middle_state = state + time_step * state_rates
        half_state = state + 0.5 * time_step * state_rates
        return slips, (old, middle_state, half_state, columns)

    def first_section(coef, rates_near, rest, after):
        rest = (rates_near, *rest)
        out_shape = (
            jax.ShapeDtypeStruct((2 * cells, members), jnp.bfloat16),
            jax.ShapeDtypeStruct((sides, cells, members), jnp.float32),
            jax.ShapeDtypeStruct((cells, members), jnp.float32),
        )
        return call(
            first_kernel, "first_section", (steps,),
            far_specs(coef, left, steps) + [whole(v) for v in rest] + [ANY] * len(after),
            [whole(v) for v in out_shape],
            out_shape, (coef, left, *rest, *after), flops, scratch,
        )

    def second_section(part, coef, rates_near, half_tractions, before, after):
        rest = (rates_near, half_tractions)
        return call(
            second_kernel, "second_section", (steps,),
            far_specs(coef, left, steps) + [whole(v) for v in rest]
            + [ANY] * (len(before) + len(after)),
            pl.BlockSpec((sides, members, cells), lambda k: (0, part, 0)),
            jax.ShapeDtypeStruct((sides, all_members, cells), jnp.float32),
            (coef, left, *rest, *before, *after), flops, scratch,
            {4: 0} if before else None,
        )

    def neighbours(slips):
        return [beside(slips, -1), slips, beside(slips, 1)]

    begun = [start(part) for part in range(PARTS)]
    around = [gathered(slips) for slips, _ in begun]
    near_rates = [near_part(neighbours(slips), near_blocks[0]) for slips, _ in begun]
    before = (left, columns, *near_rates, *around[1])
    coefs = [coefficients_of(around[0], planes, right, before)]
    arrived = [sent(coefs[0])]
    coefs.append(coefficients_of(around[1], planes, right, (coefs[0],)))
    arrived.append(sent(coefs[1]))
    first, beside_all = [], []
    for part in range(PARTS):
        first.append(first_section(arrived[part], near_rates[part], begun[part][1], (coefs[-1],)))
        beside_all.append(neighbours(first[part][0]))
        coefs.append(coefficients_of(gathered(first[part][0]), planes, right, beside_all[part]))
        arrived.append(sent(coefs[-1]))
    near_rates = [near_part(beside_all[part], near_blocks[0]) for part in range(PARTS)]
    after = (coefs[3], near_rates[1])
    result = second_section(0, arrived[2], near_rates[0], first[0][1], (), after)
    result = second_section(1, arrived[3], near_rates[1], first[1][1], (result,), ())
    new_state = jnp.concatenate([jnp.swapaxes(v[2], 0, 1) for v in first], axis=0)
    return (result, new_state)


def solution(mesh):
    mesh = Mesh(mesh.devices.reshape(SIDE, SIDE, SIDE, CORES), ALL)
    row, col = ("z", "y"), ("x", "core")
    placed = (
        P(None, None, ALL),
        P(None, ALL),
        P(ALL),
        P(ALL),
        P(ALL),
        P(ALL),
        P(ALL, None, None, None, None, None),
        P(row, col, None, None, None),
        P(ALL, None, None, None, None),
        P(row, col),
    )
    return jax.shard_map(
        on_device,
        mesh=mesh,
        in_specs=placed,
        out_specs=(P(None, None, ALL), P(None, ALL)),
        check_vma=False,
    )
```

time: 334 us -> 250 us (0.75)
  waiting for transfers between devices: 234 us -> 57.2 us
  Pallas kernels: 0 us -> 84.4 us
  starting transfers between devices: 27.4 us -> 87.5 us
  matrix products: 31.1 us -> 0 us
  between operations: 14.3 us -> 1.27 us
  other arithmetic: 13.1 us -> 5.29 us
    all_gather x2 -> x0, waiting for transfers between devices: 140 us -> none  [fault_rates(): gathered = lax.all_gather(slip_rates, 'row', axis=2, tiled=True)]
    pallas_call x0 -> x14, Pallas kernels: none -> 84.4 us  [call(): pl.pallas_call(kernel, grid=grid, in_specs=in_specs, out_specs=out_specs,...]
    ppermute x4 -> x20, waiting for transfers between devices: 94.2 us -> 18.6 us  [the longest x8 15.2 us: beside(): return lax.ppermute(slabs, ALL, pairs)]
    ppermute x4 -> x20, starting transfers between devices: 18.1 us -> 58.4 us  [the longest x8 39.1 us: beside(): return lax.ppermute(slabs, ALL, pairs)]
    all_to_all x2 -> x5, waiting for transfers between devices: 0.01 us -> 38.6 us  [the longest x4 38.6 us: sent(): lax.all_to_all(coef, ('y', 'x', 'core'), split_axis=0, concat_axis=0, til...]
    dot_general x6 -> x0, matrix products: 31.1 us -> none  [the longest x2 14 us: fault_rates(): jnp.einsum('bre,bkrp->kep', arrived[0], far_left[0], preferred_element_ty...]
    all_to_all x2 -> x5, starting transfers between devices: 9.13 us -> 29.1 us  [the longest x4 24.3 us: sent(): lax.all_to_all(coef, ('y', 'x', 'core'), split_axis=0, concat_axis=0, til...]
    another operation x6 -> x2, other arithmetic: 8.3 us -> 0.56 us  [the longest x1 0.55 us: on_device(): planes = jnp.stack([(place['z'] + dz) % SIDE for dz in OFFSETS])]
  transfers between devices with their start and end apart: 8 -> 25, of which waited for: 6 -> 6; matrix products, arithmetic and copies ran while one was open for 2% -> 3% of each run, Pallas kernels for 0% -> 27%
where the time goes in v1:
time: 250 us; the launch traced here: 248 us
  starting transfers between devices  87.5 us (35%)
  Pallas kernels  84.4 us (34%)
  waiting for transfers between devices  57.2 us (23%)
  local copies, waits for them, and re-layouts  12.6 us (5%)
  other arithmetic  5.29 us (2%)
    pallas_call x14, Pallas kernels, call(): pl.pallas_call(kernel, grid=grid, in_specs=in_specs, out_specs=out_specs,...  84.4 us
    ppermute x8, starting transfers between devices, beside(): return lax.ppermute(slabs, ALL, pairs)  39.1 us
    all_to_all x4, waiting for transfers between devices, sent(): lax.all_to_all(coef, ('y', 'x', 'core'), split_axis=0, concat_axis=0, til...  38.6 us
    all_to_all x4, starting transfers between devices, sent(): lax.all_to_all(coef, ('y', 'x', 'core'), split_axis=0, concat_axis=0, til...  24.3 us
    ppermute x12, starting transfers between devices, from_z(): return lax.ppermute(slabs, 'z', [((i + dz) % SIDE, i) for i in range(SIDE)])  19.3 us
    ppermute x8, waiting for transfers between devices, beside(): return lax.ppermute(slabs, ALL, pairs)  15.2 us
    unnamed x73, local copies, waits for them, and re-layouts  10.3 us
  transfers between devices with their start and end apart: 25, of which 6 were waited for; matrix products, arithmetic and copies ran while one was open for 3% of the time, Pallas kernels for 27%

profile of v1, /device:TPU:32, one launch (start us, length us, event | category | flops | bytes accessed | tf_op | source)
XLA Modules:
  0.0 248.3 jit_solution(1231165832758389168)
XLA Ops:
  2.0 4.8 %mask.1 = bf16[4,4,2,8,32,256]{5,4,3,2,1,0:T(8,128)(2,1)} custom-call(s32[8,16]{1,0:T(8,128)} %fusion.20.used, bf16[8,4,4,2,32,256]{5,4,3,2,1,0:T(8,128)(2,1)} %bitcast.155), custom_call_target="tpu_custom_call" | custom-call | bytes 8388608 | tf_op jit(solution)/shard_map/mask/pallas_call | solution.py:57
  6.9 4.9 %all-to-all-start = ((bf16[4,4,2,8,32,256]{5,4,3,2,1,0:T(8,128)(2,1)}), bf16[4,4,2,8,32,256]{5,4,3,2,1,0:T(8,128)(2,1)}, u32[]{:S(2)}, u32[]{:S(2)}) async-start(bf16[4,4,2,8,32,256]{5,4,3,2,1,0:T(8,128)(2,1)} %mask.1), calls=%async_computation | async-start | bytes 8388608 | tf_op jit(solution)/shard_map/all_to_all | solution.py:261
  19.8 7.9 %collective-permute-start.9 = (bf16[512,256]{1,0:T(8,128)(2,1)S(1)}, bf16[512,256]{1,0:T(8,128)(2,1)S(1)}, u32[]{:S(2)}, u32[]{:S(2)}) collective-permute-start(bf16[512,256]{1,0:T(8,128)(2,1)S(1)} %pad_maximum_fusion.1.x1.refs_9_.refs_0_), channel_id=1, source_target_pairs={{1,0},{2,1},{3,2},{4,3},{5,4},{6,5},{7,6},{8,7},{9,8},{10,9},{11,1... | collective-permute-start | bytes 786440 | tf_op jit(solution)/shard_map/ppermute | solution.py:45
  29.7 7.9 %collective-permute-start.7 = (bf16[512,256]{1,0:T(8,128)(2,1)S(1)}, bf16[512,256]{1,0:T(8,128)(2,1)S(1)}, u32[]{:S(2)}, u32[]{:S(2)}) collective-permute-start(bf16[512,256]{1,0:T(8,128)(2,1)S(1)} %pad_maximum_fusion.2.x1.refs_0_), channel_id=1, source_target_pairs={{1,0},{2,1},{3,2},{4,3},{5,4},{6,5},{7,6},{8,7},{9,8},{10,9},{11,1... | collective-permute-start | bytes 786440 | tf_op jit(solution)/shard_map/ppermute | solution.py:45
  39.7 4.2 %collective-permute-start.2 = (bf16[512,256]{1,0:T(8,128)(2,1)S(1)}, bf16[512,256]{1,0:T(8,128)(2,1)S(1)}, u32[]{:S(2)}, u32[]{:S(2)}) collective-permute-start(bf16[512,256]{1,0:T(8,128)(2,1)S(1)} %pad_maximum_fusion.1.x1.refs_9_.refs_0_), channel_id=1, source_target_pairs={{64,0},{96,32},{0,64},{32,96},{65,1},{97,33},{1,65},{33,97},{66,2}... | collective-permute-start | bytes 786440 | tf_op jit(solution)/shard_map/ppermute | solution.py:49
  51.5 13.1 %turn.1.refs_5_.weights = bf16[768,4096]{1,0:T(8,128)(2,1)} custom-call(bf16[8,4,4,3,32,256]{5,4,3,2,1,0:T(8,128)(2,1)} %bitcast.154), custom_call_target="tpu_custom_call" | custom-call | bytes 8388608 | tf_op jit(solution)/shard_map/turn/pallas_call | solution.py:57
  70.1 4.0 %near.4.refs_7_ = f32[768,256]{1,0:T(8,128)} custom-call(bf16[512,256]{1,0:T(8,128)(2,1)} %copy-done.28, bf16[512,256]{1,0:T(8,128)(2,1)} %copy-done.6, bf16[512,256]{1,0:T(8,128)(2,1)} %copy-done.29, bf16[3,3,2,256,256]{4,3,2,1,0:T(8,128)(2,1)} %bitcast.136), custom_call_target="tpu_custom_call" | custom-call | flops 603979776 | bytes 8388608 | tf_op jit(solution)/shard_map/near/pallas_call | solution.py:57
  75.2 5.3 %coefficients.4.refs_5_ = bf16[32,4,32,256]{3,2,1,0:T(8,128)(2,1)} custom-call(s32[4]{0:T(128)} %pad_add_fusion.planes, bf16[512,256]{1,0:T(8,128)(2,1)} %copy-done.6, bf16[512,256]{1,0:T(8,128)(2,1)} %copy-done.15, bf16[512,256]{1,0:T(8,128)(2,1)} %copy-done.16, bf16[512,256]{1,0:T(8,128)(2,1)} %copy-done.17, ...), custom_call_target="tpu_custom_call" | custom-call | flops 1073741824 | bytes 8388608 | tf_op jit(solution)/shard_map/coefficients/pallas_call | solution.py:57
  80.5 6.4 %all-to-all-start.2 = ((bf16[32,128,256]{2,1,0:T(8,128)(2,1)}), bf16[32,128,256]{2,1,0:T(8,128)(2,1)S(1)}, u32[]{:S(2)}, u32[]{:S(2)}) async-start(bf16[32,128,256]{2,1,0:T(8,128)(2,1)} %bitcast.140), calls=%async_computation.2 | async-start | bytes 4194304 | tf_op jit(solution)/shard_map/all_to_all | solution.py:272
  86.8 5.3 %coefficients.5.refs_0_ = bf16[32,4,32,256]{3,2,1,0:T(8,128)(2,1)} custom-call(s32[4]{0:T(128)} %pad_add_fusion.planes, bf16[512,256]{1,0:T(8,128)(2,1)} %copy-done.5, bf16[512,256]{1,0:T(8,128)(2,1)} %copy-done.7, bf16[512,256]{1,0:T(8,128)(2,1)} %copy-done.8, bf16[512,256]{1,0:T(8,128)(2,1)} %copy-done.9, ...), custom_call_target="tpu_custom_call" | custom-call | flops 1073741824 | bytes 8388608 | tf_op jit(solution)/shard_map/coefficients/pallas_call | solution.py:57
  92.2 24.7 %all-to-all-done.2 = bf16[32,128,256]{2,1,0:T(8,128)(2,1)S(1)} async-done(((bf16[32,128,256]{2,1,0:T(8,128)(2,1)}), bf16[32,128,256]{2,1,0:T(8,128)(2,1)S(1)}, u32[]{:S(2)}, u32[]{:S(2)}) %all-to-all-start.2) | async-done | bytes 2097184 | tf_op jit(solution)/shard_map/all_to_all | solution.py:272
  122.3 7.7 %first_section.2 = (bf16[512,256]{1,0:T(8,128)(2,1)}, f32[3,256,256]{2,1,0:T(8,128)}, f32[256,256]{1,0:T(8,128)}) custom-call(bf16[4096,256]{1,0:T(8,128)(2,1)} %bitcast.153, bf16[768,4096]{1,0:T(8,128)(2,1)} %turn.1.refs_5_.weights, f32[768,256]{1,0:T(8,128)} %near.4.refs_7_, f32[3,256,256]{2,1,0:T(8,128)} %bitcast.150, ...), custom_call_target="tpu_custom_call" | custom-call | flops 1610612736 | bytes 8388608 | tf_op jit(solution)/shard_map/first_section/pallas_call | solution.py:57
  135.1 7.9 %collective-permute-start.14 = (bf16[512,256]{1,0:T(8,128)(2,1)}, bf16[512,256]{1,0:T(8,128)(2,1)S(1)}, u32[]{:S(2)}, u32[]{:S(2)}) collective-permute-start(bf16[512,256]{1,0:T(8,128)(2,1)} %get-tuple-element.8.refs_0_.refs_6_.x1), channel_id=1, source_target_pairs={{1,0},{2,1},{3,2},{4,3},{5,4},{6,5},{7,6},{8,7},{9,8},{10,9},{11,1... | collective-permute-start | bytes 786440 | tf_op jit(solution)/shard_map/ppermute | solution.py:45
  144.1 6.5 %collective-permute-done.13.refs_5_.x0 = bf16[512,256]{1,0:T(8,128)(2,1)S(1)} collective-permute-done((bf16[512,256]{1,0:T(8,128)(2,1)}, bf16[512,256]{1,0:T(8,128)(2,1)S(1)}, u32[]{:S(2)}, u32[]{:S(2)}) %collective-permute-start.13) | collective-permute-done | bytes 262176 | tf_op jit(solution)/shard_map/ppermute | solution.py:45
  152.1 5.3 %coefficients.6.refs_0_ = bf16[32,4,32,256]{3,2,1,0:T(8,128)(2,1)} custom-call(s32[4]{0:T(128)} %pad_add_fusion.planes, bf16[512,256]{1,0:T(8,128)(2,1)} %get-tuple-element.8.refs_0_.refs_6_.x1, bf16[512,256]{1,0:T(8,128)(2,1)} %copy-done.18, bf16[512,256]{1,0:T(8,128)(2,1)} %copy-done.19, bf16[512,256]{1,0:T(8,128)(2,1)} %copy-done.20, ...), custom_call_target="tpu_custom_call" | custom-call | flops 1073741824 | bytes 8388608 | tf_op jit(solution)/shard_map/coefficients/pallas_call | solution.py:57
  158.7 7.3 %all-to-all-start.4 = ((bf16[32,128,256]{2,1,0:T(8,128)(2,1)}), bf16[32,128,256]{2,1,0:T(8,128)(2,1)S(1)}, u32[]{:S(2)}, u32[]{:S(2)}) async-start(bf16[32,128,256]{2,1,0:T(8,128)(2,1)} %bitcast.141), calls=%async_computation.4 | async-start | bytes 4194304 | tf_op jit(solution)/shard_map/all_to_all | solution.py:272
  166.0 7.6 %first_section.3 = (bf16[512,256]{1,0:T(8,128)(2,1)}, f32[3,256,256]{2,1,0:T(8,128)}, f32[256,256]{1,0:T(8,128)}) custom-call(bf16[4096,256]{1,0:T(8,128)(2,1)} %bitcast.152, bf16[768,4096]{1,0:T(8,128)(2,1)} %turn.1.refs_5_.weights, f32[768,256]{1,0:T(8,128)} %near.5.refs_8_, f32[3,256,256]{2,1,0:T(8,128)} %bitcast.146, ...), custom_call_target="tpu_custom_call" | custom-call | flops 1610612736 | bytes 8388608 | tf_op jit(solution)/shard_map/first_section/pallas_call | solution.py:57
  175.6 7.8 %collective-permute-start.19 = (bf16[512,256]{1,0:T(8,128)(2,1)}, bf16[512,256]{1,0:T(8,128)(2,1)S(1)}, u32[]{:S(2)}, u32[]{:S(2)}) collective-permute-start(bf16[512,256]{1,0:T(8,128)(2,1)} %get-tuple-element.9.refs_0_.refs_6_.x1), channel_id=1, source_target_pairs={{1,0},{2,1},{3,2},{4,3},{5,4},{6,5},{7,6},{8,7},{9,8},{10,9},{11,1... | collective-permute-start | bytes 786440 | tf_op jit(solution)/shard_map/ppermute | solution.py:45
  188.0 8.6 %collective-permute-done.18.refs_5_.x0 = bf16[512,256]{1,0:T(8,128)(2,1)S(1)} collective-permute-done((bf16[512,256]{1,0:T(8,128)(2,1)}, bf16[512,256]{1,0:T(8,128)(2,1)S(1)}, u32[]{:S(2)}, u32[]{:S(2)}) %collective-permute-start.18) | collective-permute-done | bytes 262176 | tf_op jit(solution)/shard_map/ppermute | solution.py:45
  198.3 5.3 %coefficients.7.refs_0_ = bf16[32,4,32,256]{3,2,1,0:T(8,128)(2,1)} custom-call(s32[4]{0:T(128)} %pad_add_fusion.planes, bf16[512,256]{1,0:T(8,128)(2,1)} %get-tuple-element.9.refs_0_.refs_6_.x1, bf16[512,256]{1,0:T(8,128)(2,1)} %copy-done.21, bf16[512,256]{1,0:T(8,128)(2,1)} %copy-done.22, bf16[512,256]{1,0:T(8,128)(2,1)} %copy-done.23, ...), custom_call_target="tpu_custom_call" | custom-call | flops 1073741824 | bytes 8388608 | tf_op jit(solution)/shard_map/coefficients/pallas_call | solution.py:57
  204.9 6.6 %all-to-all-start.3 = ((bf16[32,128,256]{2,1,0:T(8,128)(2,1)}), bf16[32,128,256]{2,1,0:T(8,128)(2,1)}, u32[]{:S(2)}, u32[]{:S(2)}) async-start(bf16[32,128,256]{2,1,0:T(8,128)(2,1)} %bitcast.142), calls=%async_computation.3 | async-start | bytes 4194304 | tf_op jit(solution)/shard_map/all_to_all | solution.py:272
  220.6 6.9 %second_section.2.refs_0_ = f32[3,512,256]{2,1,0:T(8,128)} custom-call(bf16[4096,256]{1,0:T(8,128)(2,1)} %bitcast.151, bf16[768,4096]{1,0:T(8,128)(2,1)} %turn.1.refs_5_.weights, f32[768,256]{1,0:T(8,128)} %near.7, f32[3,256,256]{2,1,0:T(8,128)} %get-tuple-element.11.half_tractions, bf16[32,4,32,256]{3,2,1,0:T(8,128)(2,1)} %coefficients.7.refs_0_, ...), custom_call_target="tpu_custom_call" | custom-call | flops 1610612736 | bytes 8388608 | tf_op jit(solution)/shard_map/second_section/pallas_call | solution.py:57
  227.5 13.9 %all-to-all-done.3 = bf16[32,128,256]{2,1,0:T(8,128)(2,1)} async-done(((bf16[32,128,256]{2,1,0:T(8,128)(2,1)}), bf16[32,128,256]{2,1,0:T(8,128)(2,1)}, u32[]{:S(2)}, u32[]{:S(2)}) %all-to-all-start.3) | async-done | bytes 2097184 | tf_op jit(solution)/shard_map/all_to_all | solution.py:272
  241.5 6.9 %second_section.3 = f32[3,512,256]{2,1,0:T(8,128)} custom-call(bf16[4096,256]{1,0:T(8,128)(2,1)} %bitcast.26.coef, bf16[768,4096]{1,0:T(8,128)(2,1)} %turn.1.refs_5_.weights, f32[768,256]{1,0:T(8,128)} %near.6.refs_1_, f32[3,256,256]{2,1,0:T(8,128)} %get-tuple-element.10.half_tractions, ...), custom_call_target="tpu_custom_call", output_to_operand_aliasing={{}: (4, {})} | custom-call | flops 1610612736 | bytes 8388608 | tf_op jit(solution)/shard_map/second_section/pallas_call | solution.py:57
  (129 shorter events, 60.3 us)
Async XLA Ops:
  6.9 67.3 %all-to-all-start = ((bf16[4,4,2,8,32,256]{5,4,3,2,1,0:T(8,128)(2,1)}), bf16[4,4,2,8,32,256]{5,4,3,2,1,0:T(8,128)(2,1)}, u32[]{:S(2)}, u32[]{:S(2)}) async-start(bf16[4,4,2,8,32,256]{5,4,3,2,1,0:T(8,128)(2,1)} %mask.1), calls=%async_computation | async-start | bytes 8388608 | tf_op jit(solution)/shard_map/all_to_all | solution.py:261
  17.9 19.8 %collective-permute-start.8 = (bf16[512,256]{1,0:T(8,128)(2,1)S(1)}, bf16[512,256]{1,0:T(8,128)(2,1)S(1)}, u32[]{:S(2)}, u32[]{:S(2)}) collective-permute-start(bf16[512,256]{1,0:T(8,128)(2,1)S(1)} %pad_maximum_fusion.1.x1.refs_9_.refs_0_), channel_id=1, source_target_pairs={{0,1},{1,2},{2,3},{3,4},{4,5},{5,6},{6,7},{7,8},{8,9},{9,10},{10,1... | collective-permute-start | bytes 786440 | tf_op jit(solution)/shard_map/ppermute | solution.py:45
  19.8 19.9 %collective-permute-start.9 = (bf16[512,256]{1,0:T(8,128)(2,1)S(1)}, bf16[512,256]{1,0:T(8,128)(2,1)S(1)}, u32[]{:S(2)}, u32[]{:S(2)}) collective-permute-start(bf16[512,256]{1,0:T(8,128)(2,1)S(1)} %pad_maximum_fusion.1.x1.refs_9_.refs_0_), channel_id=1, source_target_pairs={{1,0},{2,1},{3,2},{4,3},{5,4},{6,5},{7,6},{8,7},{9,8},{10,9},{11,1... | collective-permute-start | bytes 786440 | tf_op jit(solution)/shard_map/ppermute | solution.py:45
  27.8 16.1 %collective-permute-start.6 = (bf16[512,256]{1,0:T(8,128)(2,1)S(1)}, bf16[512,256]{1,0:T(8,128)(2,1)S(1)}, u32[]{:S(2)}, u32[]{:S(2)}) collective-permute-start(bf16[512,256]{1,0:T(8,128)(2,1)S(1)} %pad_maximum_fusion.2.x1.refs_0_), channel_id=1, source_target_pairs={{0,1},{1,2},{2,3},{3,4},{4,5},{5,6},{6,7},{7,8},{8,9},{9,10},{10,1... | collective-permute-start | bytes 786440 | tf_op jit(solution)/shard_map/ppermute | solution.py:45
  29.7 14.2 %collective-permute-start.7 = (bf16[512,256]{1,0:T(8,128)(2,1)S(1)}, bf16[512,256]{1,0:T(8,128)(2,1)S(1)}, u32[]{:S(2)}, u32[]{:S(2)}) collective-permute-start(bf16[512,256]{1,0:T(8,128)(2,1)S(1)} %pad_maximum_fusion.2.x1.refs_0_), channel_id=1, source_target_pairs={{1,0},{2,1},{3,2},{4,3},{5,4},{6,5},{7,6},{8,7},{9,8},{10,9},{11,1... | collective-permute-start | bytes 786440 | tf_op jit(solution)/shard_map/ppermute | solution.py:45
  37.7 36.4 %collective-permute-start.1 = (bf16[512,256]{1,0:T(8,128)(2,1)S(1)}, bf16[512,256]{1,0:T(8,128)(2,1)S(1)}, u32[]{:S(2)}, u32[]{:S(2)}) collective-permute-start(bf16[512,256]{1,0:T(8,128)(2,1)S(1)} %pad_maximum_fusion.1.x1.refs_9_.refs_0_), channel_id=1, source_target_pairs={{96,0},{0,32},{32,64},{64,96},{97,1},{1,33},{33,65},{65,97},{98,2}... | collective-permute-start | bytes 786440 | tf_op jit(solution)/shard_map/ppermute | solution.py:49
  39.7 34.4 %collective-permute-start.2 = (bf16[512,256]{1,0:T(8,128)(2,1)S(1)}, bf16[512,256]{1,0:T(8,128)(2,1)S(1)}, u32[]{:S(2)}, u32[]{:S(2)}) collective-permute-start(bf16[512,256]{1,0:T(8,128)(2,1)S(1)} %pad_maximum_fusion.1.x1.refs_9_.refs_0_), channel_id=1, source_target_pairs={{64,0},{96,32},{0,64},{32,96},{65,1},{97,33},{1,65},{33,97},{66,2}... | collective-permute-start | bytes 786440 | tf_op jit(solution)/shard_map/ppermute | solution.py:49
  43.9 30.2 %collective-permute-start.3 = (bf16[512,256]{1,0:T(8,128)(2,1)S(1)}, bf16[512,256]{1,0:T(8,128)(2,1)S(1)}, u32[]{:S(2)}, u32[]{:S(2)}) collective-permute-start(bf16[512,256]{1,0:T(8,128)(2,1)S(1)} %pad_maximum_fusion.2.x1.refs_0_), channel_id=1, source_target_pairs={{32,0},{64,32},{96,64},{0,96},{33,1},{65,33},{97,65},{1,97},{34,2}... | collective-permute-start | bytes 786440 | tf_op jit(solution)/shard_map/ppermute | solution.py:49
  43.9 30.2 %collective-permute-start.4 = (bf16[512,256]{1,0:T(8,128)(2,1)S(1)}, bf16[512,256]{1,0:T(8,128)(2,1)S(1)}, u32[]{:S(2)}, u32[]{:S(2)}) collective-permute-start(bf16[512,256]{1,0:T(8,128)(2,1)S(1)} %pad_maximum_fusion.2.x1.refs_0_), channel_id=1, source_target_pairs={{96,0},{0,32},{32,64},{64,96},{97,1},{1,33},{33,65},{65,97},{98,2}... | collective-permute-start | bytes 786440 | tf_op jit(solution)/shard_map/ppermute | solution.py:49
  48.2 25.9 %collective-permute-start.5 = (bf16[512,256]{1,0:T(8,128)(2,1)S(1)}, bf16[512,256]{1,0:T(8,128)(2,1)S(1)}, u32[]{:S(2)}, u32[]{:S(2)}) collective-permute-start(bf16[512,256]{1,0:T(8,128)(2,1)S(1)} %pad_maximum_fusion.2.x1.refs_0_), channel_id=1, source_target_pairs={{64,0},{96,32},{0,64},{32,96},{65,1},{97,33},{1,65},{33,97},{66,2}... | collective-permute-start | bytes 786440 | tf_op jit(solution)/shard_map/ppermute | solution.py:49
  80.5 36.3 %all-to-all-start.2 = ((bf16[32,128,256]{2,1,0:T(8,128)(2,1)}), bf16[32,128,256]{2,1,0:T(8,128)(2,1)S(1)}, u32[]{:S(2)}, u32[]{:S(2)}) async-start(bf16[32,128,256]{2,1,0:T(8,128)(2,1)} %bitcast.140), calls=%async_computation.2 | async-start | bytes 4194304 | tf_op jit(solution)/shard_map/all_to_all | solution.py:272
  118.2 39.1 %all-to-all-start.1 = ((bf16[32,128,256]{2,1,0:T(8,128)(2,1)}), bf16[32,128,256]{2,1,0:T(8,128)(2,1)S(1)}, u32[]{:S(2)}, u32[]{:S(2)}) async-start(bf16[32,128,256]{2,1,0:T(8,128)(2,1)} %bitcast.139), calls=%async_computation.1 | async-start | bytes 4194304 | tf_op jit(solution)/shard_map/all_to_all | solution.py:272
  129.9 14.2 %collective-permute-start.10 = (bf16[512,256]{1,0:T(8,128)(2,1)}, bf16[512,256]{1,0:T(8,128)(2,1)S(1)}, u32[]{:S(2)}, u32[]{:S(2)}) collective-permute-start(bf16[512,256]{1,0:T(8,128)(2,1)} %get-tuple-element.8.refs_0_.refs_6_.x1), channel_id=1, source_target_pairs={{32,0},{64,32},{96,64},{0,96},{33,1},{65,33},{97,65},{1,97},{34,2}... | collective-permute-start | bytes 786440 | tf_op jit(solution)/shard_map/ppermute | solution.py:49
  129.9 14.2 %collective-permute-start.11 = (bf16[512,256]{1,0:T(8,128)(2,1)}, bf16[512,256]{1,0:T(8,128)(2,1)S(1)}, u32[]{:S(2)}, u32[]{:S(2)}) collective-permute-start(bf16[512,256]{1,0:T(8,128)(2,1)} %get-tuple-element.8.refs_0_.refs_6_.x1), channel_id=1, source_target_pairs={{96,0},{0,32},{32,64},{64,96},{97,1},{1,33},{33,65},{65,97},{98,2}... | collective-permute-start | bytes 786440 | tf_op jit(solution)/shard_map/ppermute | solution.py:49
  131.9 12.2 %collective-permute-start.12 = (bf16[512,256]{1,0:T(8,128)(2,1)}, bf16[512,256]{1,0:T(8,128)(2,1)S(1)}, u32[]{:S(2)}, u32[]{:S(2)}) collective-permute-start(bf16[512,256]{1,0:T(8,128)(2,1)} %get-tuple-element.8.refs_0_.refs_6_.x1), channel_id=1, source_target_pairs={{64,0},{96,32},{0,64},{32,96},{65,1},{97,33},{1,65},{33,97},{66,2}... | collective-permute-start | bytes 786440 | tf_op jit(solution)/shard_map/ppermute | solution.py:49
  133.2 17.5 %collective-permute-start.13 = (bf16[512,256]{1,0:T(8,128)(2,1)}, bf16[512,256]{1,0:T(8,128)(2,1)S(1)}, u32[]{:S(2)}, u32[]{:S(2)}) collective-permute-start(bf16[512,256]{1,0:T(8,128)(2,1)} %get-tuple-element.8.refs_0_.refs_6_.x1), channel_id=1, source_target_pairs={{0,1},{1,2},{2,3},{3,4},{4,5},{5,6},{6,7},{7,8},{8,9},{9,10},{10,1... | collective-permute-start | bytes 786440 | tf_op jit(solution)/shard_map/ppermute | solution.py:45
  135.1 15.5 %collective-permute-start.14 = (bf16[512,256]{1,0:T(8,128)(2,1)}, bf16[512,256]{1,0:T(8,128)(2,1)S(1)}, u32[]{:S(2)}, u32[]{:S(2)}) collective-permute-start(bf16[512,256]{1,0:T(8,128)(2,1)} %get-tuple-element.8.refs_0_.refs_6_.x1), channel_id=1, source_target_pairs={{1,0},{2,1},{3,2},{4,3},{5,4},{6,5},{7,6},{8,7},{9,8},{10,9},{11,1... | collective-permute-start | bytes 786440 | tf_op jit(solution)/shard_map/ppermute | solution.py:45
  158.7 44.9 %all-to-all-start.4 = ((bf16[32,128,256]{2,1,0:T(8,128)(2,1)}), bf16[32,128,256]{2,1,0:T(8,128)(2,1)S(1)}, u32[]{:S(2)}, u32[]{:S(2)}) async-start(bf16[32,128,256]{2,1,0:T(8,128)(2,1)} %bitcast.141), calls=%async_computation.4 | async-start | bytes 4194304 | tf_op jit(solution)/shard_map/all_to_all | solution.py:272
  173.6 23.0 %collective-permute-start.18 = (bf16[512,256]{1,0:T(8,128)(2,1)}, bf16[512,256]{1,0:T(8,128)(2,1)S(1)}, u32[]{:S(2)}, u32[]{:S(2)}) collective-permute-start(bf16[512,256]{1,0:T(8,128)(2,1)} %get-tuple-element.9.refs_0_.refs_6_.x1), channel_id=1, source_target_pairs={{0,1},{1,2},{2,3},{3,4},{4,5},{5,6},{6,7},{7,8},{8,9},{9,10},{10,1... | collective-permute-start | bytes 786440 | tf_op jit(solution)/shard_map/ppermute | solution.py:45
  175.6 21.0 %collective-permute-start.19 = (bf16[512,256]{1,0:T(8,128)(2,1)}, bf16[512,256]{1,0:T(8,128)(2,1)S(1)}, u32[]{:S(2)}, u32[]{:S(2)}) collective-permute-start(bf16[512,256]{1,0:T(8,128)(2,1)} %get-tuple-element.9.refs_0_.refs_6_.x1), channel_id=1, source_target_pairs={{1,0},{2,1},{3,2},{4,3},{5,4},{6,5},{7,6},{8,7},{9,8},{10,9},{11,1... | collective-permute-start | bytes 786440 | tf_op jit(solution)/shard_map/ppermute | solution.py:45
  183.4 13.2 %collective-permute-start.15 = (bf16[512,256]{1,0:T(8,128)(2,1)}, bf16[512,256]{1,0:T(8,128)(2,1)S(1)}, u32[]{:S(2)}, u32[]{:S(2)}) collective-permute-start(bf16[512,256]{1,0:T(8,128)(2,1)} %get-tuple-element.9.refs_0_.refs_6_.x1), channel_id=1, source_target_pairs={{32,0},{64,32},{96,64},{0,96},{33,1},{65,33},{97,65},{1,97},{34,2}... | collective-permute-start | bytes 786440 | tf_op jit(solution)/shard_map/ppermute | solution.py:49
  183.5 13.1 %collective-permute-start.16 = (bf16[512,256]{1,0:T(8,128)(2,1)}, bf16[512,256]{1,0:T(8,128)(2,1)S(1)}, u32[]{:S(2)}, u32[]{:S(2)}) collective-permute-start(bf16[512,256]{1,0:T(8,128)(2,1)} %get-tuple-element.9.refs_0_.refs_6_.x1), channel_id=1, source_target_pairs={{96,0},{0,32},{32,64},{64,96},{97,1},{1,33},{33,65},{65,97},{98,2}... | collective-permute-start | bytes 786440 | tf_op jit(solution)/shard_map/ppermute | solution.py:49
  185.5 11.1 %collective-permute-start.17 = (bf16[512,256]{1,0:T(8,128)(2,1)}, bf16[512,256]{1,0:T(8,128)(2,1)S(1)}, u32[]{:S(2)}, u32[]{:S(2)}) collective-permute-start(bf16[512,256]{1,0:T(8,128)(2,1)} %get-tuple-element.9.refs_0_.refs_6_.x1), channel_id=1, source_target_pairs={{64,0},{96,32},{0,64},{32,96},{65,1},{97,33},{1,65},{33,97},{66,2}... | collective-permute-start | bytes 786440 | tf_op jit(solution)/shard_map/ppermute | solution.py:49
  204.9 36.6 %all-to-all-start.3 = ((bf16[32,128,256]{2,1,0:T(8,128)(2,1)}), bf16[32,128,256]{2,1,0:T(8,128)(2,1)}, u32[]{:S(2)}, u32[]{:S(2)}) async-start(bf16[32,128,256]{2,1,0:T(8,128)(2,1)} %bitcast.142), calls=%async_computation.3 | async-start | bytes 4194304 | tf_op jit(solution)/shard_map/all_to_all | solution.py:272
  (35 other events, 276.4 us)

commit v2 on v1

--- a/solution.py
+++ b/solution.py
@@ -15,7 +15,7 @@
 CORES = 2
 OFFSETS = (0, 1, 3, 2)
 ALL = ("z", "y", "x", "core")
-VMEM = 60 * 2**20
+VMEM = 65_000_000
 ANY = pl.BlockSpec(memory_space=pl.ANY)
 NT = (((1,), (1,)), ((), ()))
 
@@ -68,32 +68,37 @@
     )(*args)
 
 
-def mask_kernel(used, right, out):
-    rows, _, columns, _, width, _ = right.shape
+def mask_kernel(place, ranks, right, out):
+    rows, _, lines, _, width, _ = right.shape
     zb = pl.program_id(0)
+    first_row, col = place[0] * rows, place[1]
     slot = lax.broadcasted_iota(jnp.int32, right.shape[4:], 0)
-    for yb in range(columns):
+    for yb in range(lines):
+        b = zb * lines + yb
         for a in range(rows):
-            active = slot < used[a, zb * columns + yb]
+            near = jnp.abs(first_row + a - (b * rows + col)) < 2
+            used = jnp.where(near, 0, ranks[a, b])
             for s in range(2):
                 value = right[a, 0, yb, s]
-                out[yb, 0, s, a] = jnp.where(active, value, jnp.zeros_like(value))
-
-
-def masked_right(far_right, used):
+                out[yb, 0, s, a] = jnp.where(slot < used, value, jnp.zeros_like(value))
+
+
+def masked_right(far_right, ranks, place):
     rows, _, _, width, cells = far_right.shape
     right = far_right.reshape(rows, SIDE, SIDE, 2, width, cells)
+    scalars = pl.BlockSpec(memory_space=pltpu.SMEM)
     return call(
         mask_kernel,
         "mask",
         (SIDE,),
         [
-            pl.BlockSpec(memory_space=pltpu.SMEM),
+            scalars,
+            scalars,
             pl.BlockSpec((rows, 1, SIDE, 2, width, cells), lambda z: (0, z, 0, 0, 0, 0)),
         ],
         pl.BlockSpec((SIDE, 1, 2, rows, width, cells), lambda z: (0, z, 0, 0, 0, 0)),
         jax.ShapeDtypeStruct((SIDE, SIDE, 2, rows, width, cells), far_right.dtype),
-        (used, right),
+        (place, ranks, right),
         0,
     )
 
@@ -195,11 +200,23 @@
         new_state[...] = half_state[...] + 0.5 * time_step * state_rates
 
 
-def second_kernel(coef, weights, near, half_tractions, *refs):
+def second_kernel(coef, weights, x0, x1, x2, near_blocks, half_tractions, *refs):
     new_tractions, total = refs[-2:]
     sides, cells, _ = half_tractions.shape
-
-    @pl.when(add_far(coef, weights, near, total))
+    part = jnp.dot(weights[...], coef[...], preferred_element_type=jnp.float32)
+    step = pl.program_id(0)
+
+    @pl.when(step == 0)
+    def _():
+        for c in range(sides):
+            here = slice(c * cells, (c + 1) * cells)
+            total[here] = near_product((x0, x1, x2), near_blocks, c) + part[here]
+
+    @pl.when(step > 0)
+    def _():
+        total[...] += part
+
+    @pl.when(step == pl.num_programs(0) - 1)
     def _():
         for c in range(sides):
             rates = total[c * cells : (c + 1) * cells]
@@ -214,17 +231,20 @@
     ]
 
 
-def near_kernel(x0, x1, x2, weights, out):
-    cells = weights.shape[3]
+def near_product(slabs, weights, c):
     total = None
-    for k, x in enumerate((x0, x1, x2)):
+    for k, x in enumerate(slabs):
         part = jnp.dot(
-            jnp.concatenate([weights[k, 0, s] for s in range(2)], axis=1),
+            jnp.concatenate([weights[k, c, s] for s in range(2)], axis=1),
             x[...],
             preferred_element_type=jnp.float32,
         )
         total = part if total is None else total + part
-    out[...] = total
+    return total
+
+
+def near_kernel(x0, x1, x2, weights, out):
+    out[...] = near_product((x0, x1, x2), weights, 0)
 
 
 def near_part(slabs, near_blocks):
@@ -249,15 +269,12 @@
     place = {axis: lax.axis_index(axis) for axis in ALL}
     row = place["z"] * SIDE + place["y"]
     col = place["x"] * CORES + place["core"]
-    tile_rows, tile_cols, _, width, cells = far_right.shape
+    cells = far_right.shape[-1]
     all_members = log_state.shape[0]
     members = all_members // PARTS
     sides = far_left.shape[2]
 
-    block_row = row * tile_rows + jnp.arange(tile_rows, dtype=jnp.int32)
-    block_col = jnp.arange(tile_cols, dtype=jnp.int32) * tile_rows + col
-    near = jnp.abs(block_row[:, None] - block_col[None, :]) < 2
-    right = masked_right(far_right, jnp.where(near, 0, ranks))
+    right = masked_right(far_right, ranks, jnp.stack([row, col]))
     right = lax.all_to_all(right, "y", split_axis=0, concat_axis=0, tiled=True)
     left = turned_left(far_left[0])
     columns = jnp.stack([rate_coef, state_coef, normal_stress, inv_length], axis=1)
@@ -301,8 +318,8 @@
             out_shape, (coef, left, *rest, *after), flops, scratch,
         )
 
-    def second_section(part, coef, rates_near, half_tractions, before, after):
-        rest = (rates_near, half_tractions)
+    def second_section(part, coef, slabs, half_tractions, before, after):
+        rest = (*slabs, near_blocks[0], half_tractions)
         return call(
             second_kernel, "second_section", (steps,),
             far_specs(coef, left, steps) + [whole(v) for v in rest]
@@ -310,7 +327,7 @@
             pl.BlockSpec((sides, members, cells), lambda k: (0, part, 0)),
             jax.ShapeDtypeStruct((sides, all_members, cells), jnp.float32),
             (coef, left, *rest, *before, *after), flops, scratch,
-            {4: 0} if before else None,
+            {7: 0} if before else None,
         )
 
     def neighbours(slips):
@@ -324,16 +341,15 @@
     arrived = [sent(coefs[0])]
     coefs.append(coefficients_of(around[1], planes, right, (coefs[0],)))
     arrived.append(sent(coefs[1]))
-    first, beside_all = [], []
+    first, slabs = [], []
     for part in range(PARTS):
         first.append(first_section(arrived[part], near_rates[part], begun[part][1], (coefs[-1],)))
-        beside_all.append(neighbours(first[part][0]))
-        coefs.append(coefficients_of(gathered(first[part][0]), planes, right, beside_all[part]))
+        slabs.append(neighbours(first[part][0]))
+        early = slabs[0] if part == 0 else ()
+        coefs.append(coefficients_of(gathered(first[part][0]), planes, right, early))
         arrived.append(sent(coefs[-1]))
-    near_rates = [near_part(beside_all[part], near_blocks[0]) for part in range(PARTS)]
-    after = (coefs[3], near_rates[1])
-    result = second_section(0, arrived[2], near_rates[0], first[0][1], (), after)
-    result = second_section(1, arrived[3], near_rates[1], first[1][1], (result,), ())
+    result = second_section(0, arrived[2], slabs[0], first[0][1], (), (coefs[3],))
+    result = second_section(1, arrived[3], slabs[1], first[1][1], (result,), ())
     new_state = jnp.concatenate([jnp.swapaxes(v[2], 0, 1) for v in first], axis=0)
     return (result, new_state)
 

time: 250 us -> 244 us (0.976)
  Pallas kernels: 84.4 us -> 79.2 us
  local copies, waits for them, and re-layouts: 12.6 us -> 8.12 us
  waiting for transfers between devices: 57.2 us -> 60.7 us
    all_to_all x4, waiting for transfers between devices: 38.6 us -> 25.2 us  [sent(): lax.all_to_all(coef, ('y', 'x', 'core'), split_axis=0, concat_axis=0, til...]
    ppermute x12, waiting for transfers between devices: 3.47 us -> 15.3 us  [from_z(): return lax.ppermute(slabs, 'z', [((i + dz) % SIDE, i) for i in range(SIDE)])]
    pallas_call x14 -> x12, Pallas kernels: 84.4 us -> 79.2 us  [call(): pl.pallas_call(kernel, grid=grid, in_specs=in_specs, out_specs=out_specs,...]
    ppermute x8, waiting for transfers between devices: 15.2 us -> 20.2 us  [beside(): return lax.ppermute(slabs, ALL, pairs)]
    unnamed x73 -> x67, local copies, waits for them, and re-layouts: 10.3 us -> 5.78 us
  transfers between devices with their start and end apart: 25 -> 25, of which waited for: 6 -> 9; matrix products, arithmetic and copies ran while one was open for 3% -> 3% of each run, Pallas kernels for 27% -> 25%
where the time goes in v2:
time: 244 us; the launch traced here: 242 us
  starting transfers between devices  88.6 us (36%)
  Pallas kernels  79.2 us (32%)
  waiting for transfers between devices  60.7 us (25%)
  local copies, waits for them, and re-layouts  8.12 us (3%)
  other arithmetic  4.59 us (2%)
    pallas_call x12, Pallas kernels, call(): pl.pallas_call(kernel, grid=grid, in_specs=in_specs, out_specs=out_specs,...  79.2 us
    ppermute x8, starting transfers between devices, beside(): return lax.ppermute(slabs, ALL, pairs)  39.8 us
    all_to_all x4, starting transfers between devices, sent(): lax.all_to_all(coef, ('y', 'x', 'core'), split_axis=0, concat_axis=0, til...  25.4 us
    all_to_all x4, waiting for transfers between devices, sent(): lax.all_to_all(coef, ('y', 'x', 'core'), split_axis=0, concat_axis=0, til...  25.2 us
    ppermute x8, waiting for transfers between devices, beside(): return lax.ppermute(slabs, ALL, pairs)  20.2 us
    ppermute x12, starting transfers between devices, from_z(): return lax.ppermute(slabs, 'z', [((i + dz) % SIDE, i) for i in range(SIDE)])  18.4 us
    ppermute x12, waiting for transfers between devices, from_z(): return lax.ppermute(slabs, 'z', [((i + dz) % SIDE, i) for i in range(SIDE)])  15.3 us
    unnamed x67, local copies, waits for them, and re-layouts  5.78 us
  transfers between devices with their start and end apart: 25, of which 9 were waited for; matrix products, arithmetic and copies ran while one was open for 3% of the time, Pallas kernels for 25%

profile of v2, /device:TPU:32, one launch (start us, length us, event | category | flops | bytes accessed | tf_op | source)
XLA Modules:
  0.0 242.3 jit_solution(7087268981270559052)
XLA Ops:
  1.3 4.9 %mask.1 = bf16[4,4,2,8,32,256]{5,4,3,2,1,0:T(8,128)(2,1)} custom-call(s32[2]{0:T(128)} %pad_add_fusion.1.place, s32[8,16]{1,0:T(8,128)} %ranks.1, bf16[8,4,4,2,32,256]{5,4,3,2,1,0:T(8,128)(2,1)} %bitcast.154), custom_call_target="tpu_custom_call" | custom-call | bytes 8388608 | tf_op jit(solution)/shard_map/mask/pallas_call | solution.py:57
  6.2 5.0 %all-to-all-start = ((bf16[4,4,2,8,32,256]{5,4,3,2,1,0:T(8,128)(2,1)}), bf16[4,4,2,8,32,256]{5,4,3,2,1,0:T(8,128)(2,1)}, u32[]{:S(2)}, u32[]{:S(2)}) async-start(bf16[4,4,2,8,32,256]{5,4,3,2,1,0:T(8,128)(2,1)} %mask.1), calls=%async_computation | async-start | bytes 8388608 | tf_op jit(solution)/shard_map/all_to_all | solution.py:278
  18.9 7.9 %collective-permute-start.9 = (bf16[512,256]{1,0:T(8,128)(2,1)S(1)}, bf16[512,256]{1,0:T(8,128)(2,1)S(1)}, u32[]{:S(2)}, u32[]{:S(2)}) collective-permute-start(bf16[512,256]{1,0:T(8,128)(2,1)S(1)} %pad_maximum_fusion.1.x1.refs_9_.refs_0_), channel_id=1, source_target_pairs={{1,0},{2,1},{3,2},{4,3},{5,4},{6,5},{7,6},{8,7},{9,8},{10,9},{11,1... | collective-permute-start | bytes 786440 | tf_op jit(solution)/shard_map/ppermute | solution.py:45
  28.8 7.9 %collective-permute-start.7 = (bf16[512,256]{1,0:T(8,128)(2,1)S(1)}, bf16[512,256]{1,0:T(8,128)(2,1)S(1)}, u32[]{:S(2)}, u32[]{:S(2)}) collective-permute-start(bf16[512,256]{1,0:T(8,128)(2,1)S(1)} %pad_maximum_fusion.2.x1.refs_0_), channel_id=1, source_target_pairs={{1,0},{2,1},{3,2},{4,3},{5,4},{6,5},{7,6},{8,7},{9,8},{10,9},{11,1... | collective-permute-start | bytes 786440 | tf_op jit(solution)/shard_map/ppermute | solution.py:45
  50.5 13.1 %turn.1.refs_5_.weights = bf16[768,4096]{1,0:T(8,128)(2,1)} custom-call(bf16[8,4,4,3,32,256]{5,4,3,2,1,0:T(8,128)(2,1)} %bitcast.153), custom_call_target="tpu_custom_call" | custom-call | bytes 8388608 | tf_op jit(solution)/shard_map/turn/pallas_call | solution.py:57
  74.2 5.3 %coefficients.4.refs_5_ = bf16[32,4,32,256]{3,2,1,0:T(8,128)(2,1)} custom-call(s32[4]{0:T(128)} %pad_add_fusion.planes, bf16[512,256]{1,0:T(8,128)(2,1)} %copy-done.3, bf16[512,256]{1,0:T(8,128)(2,1)} %copy-done.11, bf16[512,256]{1,0:T(8,128)(2,1)} %copy-done.12, bf16[512,256]{1,0:T(8,128)(2,1)} %collective-permute-done.5.refs_3_, ...), custom_call_target="tpu_custom_call" | custom-call | flops 1073741824 | bytes 8388608 | tf_op jit(solution)/shard_map/coefficients/pallas_call | solution.py:57
  79.5 6.5 %all-to-all-start.2 = ((bf16[32,128,256]{2,1,0:T(8,128)(2,1)}), bf16[32,128,256]{2,1,0:T(8,128)(2,1)}, u32[]{:S(2)}, u32[]{:S(2)}) async-start(bf16[32,128,256]{2,1,0:T(8,128)(2,1)} %bitcast.142), calls=%async_computation.2 | async-start | bytes 4194304 | tf_op jit(solution)/shard_map/all_to_all | solution.py:289
  86.0 5.4 %coefficients.5.refs_0_ = bf16[32,4,32,256]{3,2,1,0:T(8,128)(2,1)} custom-call(s32[4]{0:T(128)} %pad_add_fusion.planes, bf16[512,256]{1,0:T(8,128)(2,1)} %copy-done.2, bf16[512,256]{1,0:T(8,128)(2,1)} %copy-done.5, bf16[512,256]{1,0:T(8,128)(2,1)} %copy-done.6, bf16[512,256]{1,0:T(8,128)(2,1)} %copy-done.7, ...), custom_call_target="tpu_custom_call" | custom-call | flops 1073741824 | bytes 8388608 | tf_op jit(solution)/shard_map/coefficients/pallas_call | solution.py:57
  91.3 24.6 %all-to-all-done.2 = bf16[32,128,256]{2,1,0:T(8,128)(2,1)} async-done(((bf16[32,128,256]{2,1,0:T(8,128)(2,1)}), bf16[32,128,256]{2,1,0:T(8,128)(2,1)}, u32[]{:S(2)}, u32[]{:S(2)}) %all-to-all-start.2) | async-done | bytes 2097184 | tf_op jit(solution)/shard_map/all_to_all | solution.py:289
  115.9 4.8 %all-to-all-start.1 = ((bf16[32,128,256]{2,1,0:T(8,128)(2,1)}), bf16[32,128,256]{2,1,0:T(8,128)(2,1)}, u32[]{:S(2)}, u32[]{:S(2)}) async-start(bf16[32,128,256]{2,1,0:T(8,128)(2,1)} %bitcast.141), calls=%async_computation.1 | async-start | bytes 4194304 | tf_op jit(solution)/shard_map/all_to_all | solution.py:289
  120.7 7.7 %first_section.2 = (bf16[512,256]{1,0:T(8,128)(2,1)}, f32[3,256,256]{2,1,0:T(8,128)}, f32[256,256]{1,0:T(8,128)}) custom-call(bf16[4096,256]{1,0:T(8,128)(2,1)} %bitcast.26.coef, bf16[768,4096]{1,0:T(8,128)(2,1)} %turn.1.refs_5_.weights, f32[768,256]{1,0:T(8,128)} %near.2.refs_7_, f32[3,256,256]{2,1,0:T(8,128)} %bitcast.152, ...), custom_call_target="tpu_custom_call" | custom-call | flops 1610612736 | bytes 8388608 | tf_op jit(solution)/shard_map/first_section/pallas_call | solution.py:57
  133.6 7.9 %collective-permute-start.14 = (bf16[512,256]{1,0:T(8,128)(2,1)}, bf16[512,256]{1,0:T(8,128)(2,1)S(1)}, u32[]{:S(2)}, u32[]{:S(2)}) collective-permute-start(bf16[512,256]{1,0:T(8,128)(2,1)} %get-tuple-element.8.refs_0_.refs_6_.x1), channel_id=1, source_target_pairs={{1,0},{2,1},{3,2},{4,3},{5,4},{6,5},{7,6},{8,7},{9,8},{10,9},{11,1... | collective-permute-start | bytes 786440 | tf_op jit(solution)/shard_map/ppermute | solution.py:45
  142.5 6.8 %collective-permute-done.13.refs_5_.x0 = bf16[512,256]{1,0:T(8,128)(2,1)S(1)} collective-permute-done((bf16[512,256]{1,0:T(8,128)(2,1)}, bf16[512,256]{1,0:T(8,128)(2,1)S(1)}, u32[]{:S(2)}, u32[]{:S(2)}) %collective-permute-start.13) | collective-permute-done | bytes 262176 | tf_op jit(solution)/shard_map/ppermute | solution.py:45
  150.8 5.3 %coefficients.6.refs_0_ = bf16[32,4,32,256]{3,2,1,0:T(8,128)(2,1)} custom-call(s32[4]{0:T(128)} %pad_add_fusion.planes, bf16[512,256]{1,0:T(8,128)(2,1)} %get-tuple-element.8.refs_0_.refs_6_.x1, bf16[512,256]{1,0:T(8,128)(2,1)} %copy-done.15, bf16[512,256]{1,0:T(8,128)(2,1)} %copy-done.16, bf16[512,256]{1,0:T(8,128)(2,1)} %copy-done.17, ...), custom_call_target="tpu_custom_call" | custom-call | flops 1073741824 | bytes 8388608 | tf_op jit(solution)/shard_map/coefficients/pallas_call | solution.py:57
  156.1 7.1 %all-to-all-start.4 = ((bf16[32,128,256]{2,1,0:T(8,128)(2,1)}), bf16[32,128,256]{2,1,0:T(8,128)(2,1)}, u32[]{:S(2)}, u32[]{:S(2)}) async-start(bf16[32,128,256]{2,1,0:T(8,128)(2,1)} %bitcast.143), calls=%async_computation.4 | async-start | bytes 4194304 | tf_op jit(solution)/shard_map/all_to_all | solution.py:289
  163.2 7.6 %first_section.3 = (bf16[512,256]{1,0:T(8,128)(2,1)}, f32[3,256,256]{2,1,0:T(8,128)}, f32[256,256]{1,0:T(8,128)}) custom-call(bf16[4096,256]{1,0:T(8,128)(2,1)} %bitcast.24.coef, bf16[768,4096]{1,0:T(8,128)(2,1)} %turn.1.refs_5_.weights, f32[768,256]{1,0:T(8,128)} %near.3.refs_8_, f32[3,256,256]{2,1,0:T(8,128)} %bitcast.148, ...), custom_call_target="tpu_custom_call" | custom-call | flops 1610612736 | bytes 8388608 | tf_op jit(solution)/shard_map/first_section/pallas_call | solution.py:57
  174.4 5.1 %collective-permute-done.15.refs_1_ = bf16[512,256]{1,0:T(8,128)(2,1)S(1)} collective-permute-done((bf16[512,256]{1,0:T(8,128)(2,1)}, bf16[512,256]{1,0:T(8,128)(2,1)S(1)}, u32[]{:S(2)}, u32[]{:S(2)}) %collective-permute-start.15) | collective-permute-done | bytes 262176 | tf_op jit(solution)/shard_map/ppermute | solution.py:49
  179.5 5.1 %collective-permute-done.16.refs_2_ = bf16[512,256]{1,0:T(8,128)(2,1)S(1)} collective-permute-done((bf16[512,256]{1,0:T(8,128)(2,1)}, bf16[512,256]{1,0:T(8,128)(2,1)S(1)}, u32[]{:S(2)}, u32[]{:S(2)}) %collective-permute-start.16) | collective-permute-done | bytes 262176 | tf_op jit(solution)/shard_map/ppermute | solution.py:49
  187.1 5.3 %coefficients.7.refs_0_ = bf16[32,4,32,256]{3,2,1,0:T(8,128)(2,1)} custom-call(s32[4]{0:T(128)} %pad_add_fusion.planes, bf16[512,256]{1,0:T(8,128)(2,1)} %get-tuple-element.9.refs_0_.x1, bf16[512,256]{1,0:T(8,128)(2,1)} %copy-done.24, bf16[512,256]{1,0:T(8,128)(2,1)} %copy-done.25, bf16[512,256]{1,0:T(8,128)(2,1)} %copy-done.26, ...), custom_call_target="tpu_custom_call" | custom-call | flops 1073741824 | bytes 8388608 | tf_op jit(solution)/shard_map/coefficients/pallas_call | solution.py:57
  193.0 7.1 %all-to-all-start.3 = ((bf16[32,128,256]{2,1,0:T(8,128)(2,1)}), bf16[32,128,256]{2,1,0:T(8,128)(2,1)}, u32[]{:S(2)}, u32[]{:S(2)}) async-start(bf16[32,128,256]{2,1,0:T(8,128)(2,1)} %bitcast.144), calls=%async_computation.3 | async-start | bytes 4194304 | tf_op jit(solution)/shard_map/all_to_all | solution.py:289
  202.2 8.4 %collective-permute-start.19 = (bf16[512,256]{1,0:T(8,128)(2,1)S(1)}, bf16[512,256]{1,0:T(8,128)(2,1)S(1)}, u32[]{:S(2)}, u32[]{:S(2)}) collective-permute-start(bf16[512,256]{1,0:T(8,128)(2,1)S(1)} %copy-done.10), channel_id=1, source_target_pairs={{1,0},{2,1},{3,2},{4,3},{5,4},{6,5},{7,6},{8,7},{9,8},{10,9},{11,1... | collective-permute-start | bytes 786440 | tf_op jit(solution)/shard_map/ppermute | solution.py:45
  211.7 8.3 %second_section.2.refs_0_ = f32[3,512,256]{2,1,0:T(8,128)} custom-call(bf16[4096,256]{1,0:T(8,128)(2,1)} %bitcast.30.coef, bf16[768,4096]{1,0:T(8,128)(2,1)} %turn.1.refs_5_.weights, bf16[512,256]{1,0:T(8,128)(2,1)} %copy-done.8, bf16[512,256]{1,0:T(8,128)(2,1)} %get-tuple-element.8.refs_0_.refs_6_.x1, bf16[512,256]{1,0:T(8,128)(2,1)} %copy-done.9, ...), custom_call_target="tpu_custom_call" | custom-call | flops 1610612736 | bytes 8388608 | tf_op jit(solution)/shard_map/second_section/pallas_call | solution.py:57
  219.9 13.4 %collective-permute-done.18.x0 = bf16[512,256]{1,0:T(8,128)(2,1)S(1)} collective-permute-done((bf16[512,256]{1,0:T(8,128)(2,1)S(1)}, bf16[512,256]{1,0:T(8,128)(2,1)S(1)}, u32[]{:S(2)}, u32[]{:S(2)}) %collective-permute-start.18) | collective-permute-done | bytes 262176 | tf_op jit(solution)/shard_map/ppermute | solution.py:45
  234.1 8.3 %second_section.3 = f32[3,512,256]{2,1,0:T(8,128)} custom-call(bf16[4096,256]{1,0:T(8,128)(2,1)} %bitcast.28.coef, bf16[768,4096]{1,0:T(8,128)(2,1)} %turn.1.refs_5_.weights, bf16[512,256]{1,0:T(8,128)(2,1)} %copy-done.13, bf16[512,256]{1,0:T(8,128)(2,1)} %get-tuple-element.9.refs_0_.x1, ...), custom_call_target="tpu_custom_call", output_to_operand_aliasing={{}: (7, {})} | custom-call | flops 1610612736 | bytes 8388608 | tf_op jit(solution)/shard_map/second_section/pallas_call | solution.py:57
  (119 shorter events, 52.7 us)
Async XLA Ops:
  6.2 67.0 %all-to-all-start = ((bf16[4,4,2,8,32,256]{5,4,3,2,1,0:T(8,128)(2,1)}), bf16[4,4,2,8,32,256]{5,4,3,2,1,0:T(8,128)(2,1)}, u32[]{:S(2)}, u32[]{:S(2)}) async-start(bf16[4,4,2,8,32,256]{5,4,3,2,1,0:T(8,128)(2,1)} %mask.1), calls=%async_computation | async-start | bytes 8388608 | tf_op jit(solution)/shard_map/all_to_all | solution.py:278
  16.9 19.8 %collective-permute-start.8 = (bf16[512,256]{1,0:T(8,128)(2,1)S(1)}, bf16[512,256]{1,0:T(8,128)(2,1)S(1)}, u32[]{:S(2)}, u32[]{:S(2)}) collective-permute-start(bf16[512,256]{1,0:T(8,128)(2,1)S(1)} %pad_maximum_fusion.1.x1.refs_9_.refs_0_), channel_id=1, source_target_pairs={{0,1},{1,2},{2,3},{3,4},{4,5},{5,6},{6,7},{7,8},{8,9},{9,10},{10,1... | collective-permute-start | bytes 786440 | tf_op jit(solution)/shard_map/ppermute | solution.py:45
  18.9 19.9 %collective-permute-start.9 = (bf16[512,256]{1,0:T(8,128)(2,1)S(1)}, bf16[512,256]{1,0:T(8,128)(2,1)S(1)}, u32[]{:S(2)}, u32[]{:S(2)}) collective-permute-start(bf16[512,256]{1,0:T(8,128)(2,1)S(1)} %pad_maximum_fusion.1.x1.refs_9_.refs_0_), channel_id=1, source_target_pairs={{1,0},{2,1},{3,2},{4,3},{5,4},{6,5},{7,6},{8,7},{9,8},{10,9},{11,1... | collective-permute-start | bytes 786440 | tf_op jit(solution)/shard_map/ppermute | solution.py:45
  26.8 16.1 %collective-permute-start.6 = (bf16[512,256]{1,0:T(8,128)(2,1)S(1)}, bf16[512,256]{1,0:T(8,128)(2,1)S(1)}, u32[]{:S(2)}, u32[]{:S(2)}) collective-permute-start(bf16[512,256]{1,0:T(8,128)(2,1)S(1)} %pad_maximum_fusion.2.x1.refs_0_), channel_id=1, source_target_pairs={{0,1},{1,2},{2,3},{3,4},{4,5},{5,6},{6,7},{7,8},{8,9},{9,10},{10,1... | collective-permute-start | bytes 786440 | tf_op jit(solution)/shard_map/ppermute | solution.py:45
  28.8 14.2 %collective-permute-start.7 = (bf16[512,256]{1,0:T(8,128)(2,1)S(1)}, bf16[512,256]{1,0:T(8,128)(2,1)S(1)}, u32[]{:S(2)}, u32[]{:S(2)}) collective-permute-start(bf16[512,256]{1,0:T(8,128)(2,1)S(1)} %pad_maximum_fusion.2.x1.refs_0_), channel_id=1, source_target_pairs={{1,0},{2,1},{3,2},{4,3},{5,4},{6,5},{7,6},{8,7},{9,8},{10,9},{11,1... | collective-permute-start | bytes 786440 | tf_op jit(solution)/shard_map/ppermute | solution.py:45
  36.6 10.6 %collective-permute-start = (bf16[512,256]{1,0:T(8,128)(2,1)S(1)}, bf16[512,256]{1,0:T(8,128)(2,1)S(1)}, u32[]{:S(2)}, u32[]{:S(2)}) collective-permute-start(bf16[512,256]{1,0:T(8,128)(2,1)S(1)} %pad_maximum_fusion.1.x1.refs_9_.refs_0_), channel_id=1, source_target_pairs={{32,0},{64,32},{96,64},{0,96},{33,1},{65,33},{97,65},{1,97},{34,2}... | collective-permute-start | bytes 786440 | tf_op jit(solution)/shard_map/ppermute | solution.py:49
  36.7 36.4 %collective-permute-start.1 = (bf16[512,256]{1,0:T(8,128)(2,1)S(1)}, bf16[512,256]{1,0:T(8,128)(2,1)S(1)}, u32[]{:S(2)}, u32[]{:S(2)}) collective-permute-start(bf16[512,256]{1,0:T(8,128)(2,1)S(1)} %pad_maximum_fusion.1.x1.refs_9_.refs_0_), channel_id=1, source_target_pairs={{96,0},{0,32},{32,64},{64,96},{97,1},{1,33},{33,65},{65,97},{98,2}... | collective-permute-start | bytes 786440 | tf_op jit(solution)/shard_map/ppermute | solution.py:49
  38.7 34.4 %collective-permute-start.2 = (bf16[512,256]{1,0:T(8,128)(2,1)S(1)}, bf16[512,256]{1,0:T(8,128)(2,1)S(1)}, u32[]{:S(2)}, u32[]{:S(2)}) collective-permute-start(bf16[512,256]{1,0:T(8,128)(2,1)S(1)} %pad_maximum_fusion.1.x1.refs_9_.refs_0_), channel_id=1, source_target_pairs={{64,0},{96,32},{0,64},{32,96},{65,1},{97,33},{1,65},{33,97},{66,2}... | collective-permute-start | bytes 786440 | tf_op jit(solution)/shard_map/ppermute | solution.py:49
  42.9 30.2 %collective-permute-start.3 = (bf16[512,256]{1,0:T(8,128)(2,1)S(1)}, bf16[512,256]{1,0:T(8,128)(2,1)S(1)}, u32[]{:S(2)}, u32[]{:S(2)}) collective-permute-start(bf16[512,256]{1,0:T(8,128)(2,1)S(1)} %pad_maximum_fusion.2.x1.refs_0_), channel_id=1, source_target_pairs={{32,0},{64,32},{96,64},{0,96},{33,1},{65,33},{97,65},{1,97},{34,2}... | collective-permute-start | bytes 786440 | tf_op jit(solution)/shard_map/ppermute | solution.py:49
  43.0 30.2 %collective-permute-start.4 = (bf16[512,256]{1,0:T(8,128)(2,1)S(1)}, bf16[512,256]{1,0:T(8,128)(2,1)S(1)}, u32[]{:S(2)}, u32[]{:S(2)}) collective-permute-start(bf16[512,256]{1,0:T(8,128)(2,1)S(1)} %pad_maximum_fusion.2.x1.refs_0_), channel_id=1, source_target_pairs={{96,0},{0,32},{32,64},{64,96},{97,1},{1,33},{33,65},{65,97},{98,2}... | collective-permute-start | bytes 786440 | tf_op jit(solution)/shard_map/ppermute | solution.py:49
  47.3 25.9 %collective-permute-start.5 = (bf16[512,256]{1,0:T(8,128)(2,1)S(1)}, bf16[512,256]{1,0:T(8,128)(2,1)}, u32[]{:S(2)}, u32[]{:S(2)}) collective-permute-start(bf16[512,256]{1,0:T(8,128)(2,1)S(1)} %pad_maximum_fusion.2.x1.refs_0_), channel_id=1, source_target_pairs={{64,0},{96,32},{0,64},{32,96},{65,1},{97,33},{1,65},{33,97},{66,2}... | collective-permute-start | bytes 786440 | tf_op jit(solution)/shard_map/ppermute | solution.py:49
  79.5 36.4 %all-to-all-start.2 = ((bf16[32,128,256]{2,1,0:T(8,128)(2,1)}), bf16[32,128,256]{2,1,0:T(8,128)(2,1)}, u32[]{:S(2)}, u32[]{:S(2)}) async-start(bf16[32,128,256]{2,1,0:T(8,128)(2,1)} %bitcast.142), calls=%async_computation.2 | async-start | bytes 4194304 | tf_op jit(solution)/shard_map/all_to_all | solution.py:289
  115.9 40.1 %all-to-all-start.1 = ((bf16[32,128,256]{2,1,0:T(8,128)(2,1)}), bf16[32,128,256]{2,1,0:T(8,128)(2,1)}, u32[]{:S(2)}, u32[]{:S(2)}) async-start(bf16[32,128,256]{2,1,0:T(8,128)(2,1)} %bitcast.141), calls=%async_computation.1 | async-start | bytes 4194304 | tf_op jit(solution)/shard_map/all_to_all | solution.py:289
  128.4 14.1 %collective-permute-start.10 = (bf16[512,256]{1,0:T(8,128)(2,1)}, bf16[512,256]{1,0:T(8,128)(2,1)S(1)}, u32[]{:S(2)}, u32[]{:S(2)}) collective-permute-start(bf16[512,256]{1,0:T(8,128)(2,1)} %get-tuple-element.8.refs_0_.refs_6_.x1), channel_id=1, source_target_pairs={{32,0},{64,32},{96,64},{0,96},{33,1},{65,33},{97,65},{1,97},{34,2}... | collective-permute-start | bytes 786440 | tf_op jit(solution)/shard_map/ppermute | solution.py:49
  128.4 14.1 %collective-permute-start.11 = (bf16[512,256]{1,0:T(8,128)(2,1)}, bf16[512,256]{1,0:T(8,128)(2,1)S(1)}, u32[]{:S(2)}, u32[]{:S(2)}) collective-permute-start(bf16[512,256]{1,0:T(8,128)(2,1)} %get-tuple-element.8.refs_0_.refs_6_.x1), channel_id=1, source_target_pairs={{96,0},{0,32},{32,64},{64,96},{97,1},{1,33},{33,65},{65,97},{98,2}... | collective-permute-start | bytes 786440 | tf_op jit(solution)/shard_map/ppermute | solution.py:49
  130.4 12.1 %collective-permute-start.12 = (bf16[512,256]{1,0:T(8,128)(2,1)}, bf16[512,256]{1,0:T(8,128)(2,1)S(1)}, u32[]{:S(2)}, u32[]{:S(2)}) collective-permute-start(bf16[512,256]{1,0:T(8,128)(2,1)} %get-tuple-element.8.refs_0_.refs_6_.x1), channel_id=1, source_target_pairs={{64,0},{96,32},{0,64},{32,96},{65,1},{97,33},{1,65},{33,97},{66,2}... | collective-permute-start | bytes 786440 | tf_op jit(solution)/shard_map/ppermute | solution.py:49
  131.7 17.6 %collective-permute-start.13 = (bf16[512,256]{1,0:T(8,128)(2,1)}, bf16[512,256]{1,0:T(8,128)(2,1)S(1)}, u32[]{:S(2)}, u32[]{:S(2)}) collective-permute-start(bf16[512,256]{1,0:T(8,128)(2,1)} %get-tuple-element.8.refs_0_.refs_6_.x1), channel_id=1, source_target_pairs={{0,1},{1,2},{2,3},{3,4},{4,5},{5,6},{6,7},{7,8},{8,9},{9,10},{10,1... | collective-permute-start | bytes 786440 | tf_op jit(solution)/shard_map/ppermute | solution.py:45
  133.6 15.7 %collective-permute-start.14 = (bf16[512,256]{1,0:T(8,128)(2,1)}, bf16[512,256]{1,0:T(8,128)(2,1)S(1)}, u32[]{:S(2)}, u32[]{:S(2)}) collective-permute-start(bf16[512,256]{1,0:T(8,128)(2,1)} %get-tuple-element.8.refs_0_.refs_6_.x1), channel_id=1, source_target_pairs={{1,0},{2,1},{3,2},{4,3},{5,4},{6,5},{7,6},{8,7},{9,8},{10,9},{11,1... | collective-permute-start | bytes 786440 | tf_op jit(solution)/shard_map/ppermute | solution.py:45
  156.1 36.9 %all-to-all-start.4 = ((bf16[32,128,256]{2,1,0:T(8,128)(2,1)}), bf16[32,128,256]{2,1,0:T(8,128)(2,1)}, u32[]{:S(2)}, u32[]{:S(2)}) async-start(bf16[32,128,256]{2,1,0:T(8,128)(2,1)} %bitcast.143), calls=%async_computation.4 | async-start | bytes 4194304 | tf_op jit(solution)/shard_map/all_to_all | solution.py:289
  170.8 13.8 %collective-permute-start.16 = (bf16[512,256]{1,0:T(8,128)(2,1)}, bf16[512,256]{1,0:T(8,128)(2,1)S(1)}, u32[]{:S(2)}, u32[]{:S(2)}) collective-permute-start(bf16[512,256]{1,0:T(8,128)(2,1)} %get-tuple-element.9.refs_0_.x1), channel_id=1, source_target_pairs={{96,0},{0,32},{32,64},{64,96},{97,1},{1,33},{33,65},{65,97},{98,2}... | collective-permute-start | bytes 786440 | tf_op jit(solution)/shard_map/ppermute | solution.py:49
  173.0 13.3 %collective-permute-start.17 = (bf16[512,256]{1,0:T(8,128)(2,1)}, bf16[512,256]{1,0:T(8,128)(2,1)S(1)}, u32[]{:S(2)}, u32[]{:S(2)}) collective-permute-start(bf16[512,256]{1,0:T(8,128)(2,1)} %get-tuple-element.9.refs_0_.x1), channel_id=1, source_target_pairs={{64,0},{96,32},{0,64},{32,96},{65,1},{97,33},{1,65},{33,97},{66,2}... | collective-permute-start | bytes 786440 | tf_op jit(solution)/shard_map/ppermute | solution.py:49
  193.0 40.3 %all-to-all-start.3 = ((bf16[32,128,256]{2,1,0:T(8,128)(2,1)}), bf16[32,128,256]{2,1,0:T(8,128)(2,1)}, u32[]{:S(2)}, u32[]{:S(2)}) async-start(bf16[32,128,256]{2,1,0:T(8,128)(2,1)} %bitcast.144), calls=%async_computation.3 | async-start | bytes 4194304 | tf_op jit(solution)/shard_map/all_to_all | solution.py:289
  200.1 33.2 %collective-permute-start.18 = (bf16[512,256]{1,0:T(8,128)(2,1)S(1)}, bf16[512,256]{1,0:T(8,128)(2,1)S(1)}, u32[]{:S(2)}, u32[]{:S(2)}) collective-permute-start(bf16[512,256]{1,0:T(8,128)(2,1)S(1)} %copy-done.10), channel_id=1, source_target_pairs={{0,1},{1,2},{2,3},{3,4},{4,5},{5,6},{6,7},{7,8},{8,9},{9,10},{10,1... | collective-permute-start | bytes 786440 | tf_op jit(solution)/shard_map/ppermute | solution.py:45
  202.2 31.1 %collective-permute-start.19 = (bf16[512,256]{1,0:T(8,128)(2,1)S(1)}, bf16[512,256]{1,0:T(8,128)(2,1)S(1)}, u32[]{:S(2)}, u32[]{:S(2)}) collective-permute-start(bf16[512,256]{1,0:T(8,128)(2,1)S(1)} %copy-done.10), channel_id=1, source_target_pairs={{1,0},{2,1},{3,2},{4,3},{5,4},{6,5},{7,6},{8,7},{9,8},{10,9},{11,1... | collective-permute-start | bytes 786440 | tf_op jit(solution)/shard_map/ppermute | solution.py:45
  (32 other events, 257.4 us)

commit v3 on v2

--- a/solution.py
+++ b/solution.py
@@ -243,21 +243,23 @@
     return total
 
 
-def near_kernel(x0, x1, x2, weights, out):
+def near_kernel(x0, x1, x2, weights, *refs):
+    out = refs[-1]
     out[...] = near_product((x0, x1, x2), weights, 0)
 
 
-def near_part(slabs, near_blocks):
+def near_part(slabs, near_blocks, after):
     depth, members = slabs[0].shape
     sides, cells = near_blocks.shape[1], near_blocks.shape[3]
     return call(
         near_kernel,
         "near",
         (sides,),
-        [whole(slabs[0])] * 3 + [pl.BlockSpec((3, 1, 2, cells, cells), lambda c: (0, c, 0, 0, 0))],
+        [whole(slabs[0])] * 3 + [pl.BlockSpec((3, 1, 2, cells, cells), lambda c: (0, c, 0, 0, 0))]
+        + [ANY] * len(after),
         pl.BlockSpec((cells, members), lambda c: (c, 0)),
         jax.ShapeDtypeStruct((sides * cells, members), jnp.float32),
-        (*slabs, near_blocks),
+        (*slabs, near_blocks, *after),
         2 * 3 * sides * cells * depth * members,
     )
 
@@ -335,12 +337,13 @@
 
     begun = [start(part) for part in range(PARTS)]
     around = [gathered(slips) for slips, _ in begun]
-    near_rates = [near_part(neighbours(slips), near_blocks[0]) for slips, _ in begun]
-    before = (left, columns, *near_rates, *around[1])
+    slabs = [neighbours(slips) for slips, _ in begun]
+    before = (left, columns, *around[1])
     coefs = [coefficients_of(around[0], planes, right, before)]
     arrived = [sent(coefs[0])]
     coefs.append(coefficients_of(around[1], planes, right, (coefs[0],)))
     arrived.append(sent(coefs[1]))
+    near_rates = [near_part(v, near_blocks[0], (coefs[1],)) for v in slabs]
     first, slabs = [], []
     for part in range(PARTS):
         first.append(first_section(arrived[part], near_rates[part], begun[part][1], (coefs[-1],)))

time: 244 us -> 296 us (1.21)
  waiting for transfers between devices: 60.7 us -> 103 us
  starting transfers between devices: 88.6 us -> 98.2 us
    ppermute x8, waiting for transfers between devices: 20.2 us -> 61.2 us  [beside(): return lax.ppermute(slabs, ALL, pairs)]
    ppermute x12, starting transfers between devices: 18.4 us -> 28.5 us  [from_z(): return lax.ppermute(slabs, 'z', [((i + dz) % SIDE, i) for i in range(SIDE)])]
    all_to_all x1, waiting for transfers between devices: 0.01 us -> 9.65 us  [on_device(): right = lax.all_to_all(right, 'y', split_axis=0, concat_axis=0, tiled=True)]
    ppermute x12, waiting for transfers between devices: 15.3 us -> 7.09 us  [from_z(): return lax.ppermute(slabs, 'z', [((i + dz) % SIDE, i) for i in range(SIDE)])]
    unnamed x67 -> x71, local copies, waits for them, and re-layouts: 5.78 us -> 6.33 us
  transfers between devices with their start and end apart: 25 -> 25, of which waited for: 9 -> 11; matrix products, arithmetic and copies ran while one was open for 3% -> 3% of each run, Pallas kernels for 25% -> 21%
where the time goes in v3:
time: 296 us; the launch traced here: 294 us
  waiting for transfers between devices  103 us (35%)
  starting transfers between devices  98.2 us (33%)
  Pallas kernels  79.3 us (27%)
  local copies, waits for them, and re-layouts  8.66 us (3%)
  other arithmetic  4.64 us (2%)
    pallas_call x12, Pallas kernels, call(): pl.pallas_call(kernel, grid=grid, in_specs=in_specs, out_specs=out_specs,...  79.3 us
    ppermute x8, waiting for transfers between devices, beside(): return lax.ppermute(slabs, ALL, pairs)  61.2 us
    ppermute x8, starting transfers between devices, beside(): return lax.ppermute(slabs, ALL, pairs)  42.2 us
    ppermute x12, starting transfers between devices, from_z(): return lax.ppermute(slabs, 'z', [((i + dz) % SIDE, i) for i in range(SIDE)])  28.5 us
    all_to_all x4, waiting for transfers between devices, sent(): lax.all_to_all(coef, ('y', 'x', 'core'), split_axis=0, concat_axis=0, til...  24.6 us
    all_to_all x4, starting transfers between devices, sent(): lax.all_to_all(coef, ('y', 'x', 'core'), split_axis=0, concat_axis=0, til...  22.5 us
    all_to_all x1, waiting for transfers between devices, on_device(): right = lax.all_to_all(right, 'y', split_axis=0, concat_axis=0, tiled=True)  9.65 us
    ppermute x12, waiting for transfers between devices, from_z(): return lax.ppermute(slabs, 'z', [((i + dz) % SIDE, i) for i in range(SIDE)])  7.09 us
  transfers between devices with their start and end apart: 25, of which 11 were waited for; matrix products, arithmetic and copies ran while one was open for 3% of the time, Pallas kernels for 21%

profile of v3, /device:TPU:32, one launch (start us, length us, event | category | flops | bytes accessed | tf_op | source)
XLA Modules:
  0.0 294.5 jit_solution(17785815397691423492)
XLA Ops:
  6.2 5.0 %all-to-all-start = ((bf16[4,4,2,8,32,256]{5,4,3,2,1,0:T(8,128)(2,1)}), bf16[4,4,2,8,32,256]{5,4,3,2,1,0:T(8,128)(2,1)}, u32[]{:S(2)}, u32[]{:S(2)}) async-start(bf16[4,4,2,8,32,256]{5,4,3,2,1,0:T(8,128)(2,1)} %mask.1), calls=%async_computation | async-start | bytes 8388608 | tf_op jit(solution)/shard_map/all_to_all | solution.py:280
  25.7 10.4 %collective-permute-start.5 = (bf16[512,256]{1,0:T(8,128)(2,1)S(1)}, bf16[512,256]{1,0:T(8,128)(2,1)S(1)}, u32[]{:S(2)}, u32[]{:S(2)}) collective-permute-start(bf16[512,256]{1,0:T(8,128)(2,1)S(1)} %pad_maximum_fusion.2.refs_0_.x1), channel_id=1, source_target_pairs={{64,0},{96,32},{0,64},{32,96},{65,1},{97,33},{1,65},{33,97},{66,2}... | collective-permute-start | bytes 786440 | tf_op jit(solution)/shard_map/ppermute | solution.py:49
  36.1 13.2 %turn.1.refs_5_.weights = bf16[768,4096]{1,0:T(8,128)(2,1)} custom-call(bf16[8,4,4,3,32,256]{5,4,3,2,1,0:T(8,128)(2,1)} %bitcast.153), custom_call_target="tpu_custom_call" | custom-call | bytes 8388608 | tf_op jit(solution)/shard_map/turn/pallas_call | solution.py:57
  50.7 9.6 %all-to-all-done.refs_4_ = bf16[4,4,2,8,32,256]{5,4,3,2,1,0:T(8,128)(2,1)} async-done(((bf16[4,4,2,8,32,256]{5,4,3,2,1,0:T(8,128)(2,1)}), bf16[4,4,2,8,32,256]{5,4,3,2,1,0:T(8,128)(2,1)}, u32[]{:S(2)}, u32[]{:S(2)}) %all-to-all-start) | async-done | bytes 4194336 | tf_op jit(solution)/shard_map/all_to_all | solution.py:280
  60.4 5.4 %coefficients.4.refs_5_ = bf16[32,4,32,256]{3,2,1,0:T(8,128)(2,1)} custom-call(s32[4]{0:T(128)} %pad_add_fusion.planes, bf16[512,256]{1,0:T(8,128)(2,1)} %copy-done.4, bf16[512,256]{1,0:T(8,128)(2,1)} %copy-done.12, bf16[512,256]{1,0:T(8,128)(2,1)} %copy-done.13, bf16[512,256]{1,0:T(8,128)(2,1)} %copy-done.14, ...), custom_call_target="tpu_custom_call" | custom-call | flops 1073741824 | bytes 8388608 | tf_op jit(solution)/shard_map/coefficients/pallas_call | solution.py:57
  65.7 5.4 %all-to-all-start.2 = ((bf16[32,128,256]{2,1,0:T(8,128)(2,1)}), bf16[32,128,256]{2,1,0:T(8,128)(2,1)}, u32[]{:S(2)}, u32[]{:S(2)}) async-start(bf16[32,128,256]{2,1,0:T(8,128)(2,1)} %bitcast.144), calls=%async_computation.2 | async-start | bytes 4194304 | tf_op jit(solution)/shard_map/all_to_all | solution.py:291
  71.1 5.3 %coefficients.5.refs_0_ = bf16[32,4,32,256]{3,2,1,0:T(8,128)(2,1)} custom-call(s32[4]{0:T(128)} %pad_add_fusion.planes, bf16[512,256]{1,0:T(8,128)(2,1)} %copy-done.2, bf16[512,256]{1,0:T(8,128)(2,1)} %copy-done.7, bf16[512,256]{1,0:T(8,128)(2,1)} %copy-done.8, bf16[512,256]{1,0:T(8,128)(2,1)} %collective-permute-done.2.refs_10_.refs_3_, ...), custom_call_target="tpu_custom_call" | custom-call | flops 1073741824 | bytes 8388608 | tf_op jit(solution)/shard_map/coefficients/pallas_call | solution.py:57
  76.5 24.6 %all-to-all-done.2 = bf16[32,128,256]{2,1,0:T(8,128)(2,1)} async-done(((bf16[32,128,256]{2,1,0:T(8,128)(2,1)}), bf16[32,128,256]{2,1,0:T(8,128)(2,1)}, u32[]{:S(2)}, u32[]{:S(2)}) %all-to-all-start.2) | async-done | bytes 2097184 | tf_op jit(solution)/shard_map/all_to_all | solution.py:291
  101.1 4.9 %all-to-all-start.1 = ((bf16[32,128,256]{2,1,0:T(8,128)(2,1)}), bf16[32,128,256]{2,1,0:T(8,128)(2,1)}, u32[]{:S(2)}, u32[]{:S(2)}) async-start(bf16[32,128,256]{2,1,0:T(8,128)(2,1)} %bitcast.137), calls=%async_computation.1 | async-start | bytes 4194304 | tf_op jit(solution)/shard_map/all_to_all | solution.py:291
  108.0 7.8 %collective-permute-start.9 = (bf16[512,256]{1,0:T(8,128)(2,1)S(1)}, bf16[512,256]{1,0:T(8,128)(2,1)S(1)}, u32[]{:S(2)}, u32[]{:S(2)}) collective-permute-start(bf16[512,256]{1,0:T(8,128)(2,1)S(1)} %copy-done.5), channel_id=1, source_target_pairs={{1,0},{2,1},{3,2},{4,3},{5,4},{6,5},{7,6},{8,7},{9,8},{10,9},{11,1... | collective-permute-start | bytes 786440 | tf_op jit(solution)/shard_map/ppermute | solution.py:45
  115.8 21.2 %collective-permute-done.8.x0 = bf16[512,256]{1,0:T(8,128)(2,1)S(1)} collective-permute-done((bf16[512,256]{1,0:T(8,128)(2,1)S(1)}, bf16[512,256]{1,0:T(8,128)(2,1)S(1)}, u32[]{:S(2)}, u32[]{:S(2)}) %collective-permute-start.8) | collective-permute-done | bytes 262176 | tf_op jit(solution)/shard_map/ppermute | solution.py:45
  141.9 7.6 %first_section.2 = (bf16[512,256]{1,0:T(8,128)(2,1)}, f32[3,256,256]{2,1,0:T(8,128)}, f32[256,256]{1,0:T(8,128)}) custom-call(bf16[4096,256]{1,0:T(8,128)(2,1)} %bitcast.26.coef, bf16[768,4096]{1,0:T(8,128)(2,1)} %turn.1.refs_5_.weights, f32[768,256]{1,0:T(8,128)} %near.3, f32[3,256,256]{2,1,0:T(8,128)} %bitcast.152, ...), custom_call_target="tpu_custom_call" | custom-call | flops 1610612736 | bytes 8388608 | tf_op jit(solution)/shard_map/first_section/pallas_call | solution.py:57
  157.9 7.9 %collective-permute-start.14 = (bf16[512,256]{1,0:T(8,128)(2,1)}, bf16[512,256]{1,0:T(8,128)(2,1)S(1)}, u32[]{:S(2)}, u32[]{:S(2)}) collective-permute-start(bf16[512,256]{1,0:T(8,128)(2,1)} %get-tuple-element.8.refs_0_.refs_6_.x1), channel_id=1, source_target_pairs={{1,0},{2,1},{3,2},{4,3},{5,4},{6,5},{7,6},{8,7},{9,8},{10,9},{11,1... | collective-permute-start | bytes 786440 | tf_op jit(solution)/shard_map/ppermute | solution.py:45
  170.7 5.3 %coefficients.6.refs_0_ = bf16[32,4,32,256]{3,2,1,0:T(8,128)(2,1)} custom-call(s32[4]{0:T(128)} %pad_add_fusion.planes, bf16[512,256]{1,0:T(8,128)(2,1)} %get-tuple-element.8.refs_0_.refs_6_.x1, bf16[512,256]{1,0:T(8,128)(2,1)} %copy-done.17, bf16[512,256]{1,0:T(8,128)(2,1)} %copy-done.18, bf16[512,256]{1,0:T(8,128)(2,1)} %copy-done.19, ...), custom_call_target="tpu_custom_call" | custom-call | flops 1073741824 | bytes 8388608 | tf_op jit(solution)/shard_map/coefficients/pallas_call | solution.py:57
  176.0 5.9 %all-to-all-start.4 = ((bf16[32,128,256]{2,1,0:T(8,128)(2,1)}), bf16[32,128,256]{2,1,0:T(8,128)(2,1)}, u32[]{:S(2)}, u32[]{:S(2)}) async-start(bf16[32,128,256]{2,1,0:T(8,128)(2,1)} %bitcast.142), calls=%async_computation.4 | async-start | bytes 4194304 | tf_op jit(solution)/shard_map/all_to_all | solution.py:291
  184.1 8.8 %collective-permute-start.7 = (bf16[512,256]{1,0:T(8,128)(2,1)S(1)}, bf16[512,256]{1,0:T(8,128)(2,1)S(1)}, u32[]{:S(2)}, u32[]{:S(2)}) collective-permute-start(bf16[512,256]{1,0:T(8,128)(2,1)S(1)} %copy-done.3), channel_id=1, source_target_pairs={{1,0},{2,1},{3,2},{4,3},{5,4},{6,5},{7,6},{8,7},{9,8},{10,9},{11,1... | collective-permute-start | bytes 786440 | tf_op jit(solution)/shard_map/ppermute | solution.py:45
  192.9 22.5 %collective-permute-done.6.x0 = bf16[512,256]{1,0:T(8,128)(2,1)S(1)} collective-permute-done((bf16[512,256]{1,0:T(8,128)(2,1)S(1)}, bf16[512,256]{1,0:T(8,128)(2,1)S(1)}, u32[]{:S(2)}, u32[]{:S(2)}) %collective-permute-start.6) | collective-permute-done | bytes 262176 | tf_op jit(solution)/shard_map/ppermute | solution.py:45
  220.9 7.6 %first_section.3 = (bf16[512,256]{1,0:T(8,128)(2,1)}, f32[3,256,256]{2,1,0:T(8,128)}, f32[256,256]{1,0:T(8,128)}) custom-call(bf16[4096,256]{1,0:T(8,128)(2,1)} %bitcast.23.coef, bf16[768,4096]{1,0:T(8,128)(2,1)} %turn.1.refs_5_.weights, f32[768,256]{1,0:T(8,128)} %near.2, f32[3,256,256]{2,1,0:T(8,128)} %bitcast.148, ...), custom_call_target="tpu_custom_call" | custom-call | flops 1610612736 | bytes 8388608 | tf_op jit(solution)/shard_map/first_section/pallas_call | solution.py:57
  239.4 5.3 %coefficients.7.refs_0_ = bf16[32,4,32,256]{3,2,1,0:T(8,128)(2,1)} custom-call(s32[4]{0:T(128)} %pad_add_fusion.planes, bf16[512,256]{1,0:T(8,128)(2,1)} %get-tuple-element.9.refs_0_.x1, bf16[512,256]{1,0:T(8,128)(2,1)} %copy-done.26, bf16[512,256]{1,0:T(8,128)(2,1)} %copy-done.27, bf16[512,256]{1,0:T(8,128)(2,1)} %copy-done.28, ...), custom_call_target="tpu_custom_call" | custom-call | flops 1073741824 | bytes 8388608 | tf_op jit(solution)/shard_map/coefficients/pallas_call | solution.py:57
  244.7 6.2 %all-to-all-start.3 = ((bf16[32,128,256]{2,1,0:T(8,128)(2,1)}), bf16[32,128,256]{2,1,0:T(8,128)(2,1)}, u32[]{:S(2)}, u32[]{:S(2)}) async-start(bf16[32,128,256]{2,1,0:T(8,128)(2,1)} %bitcast.143), calls=%async_computation.3 | async-start | bytes 4194304 | tf_op jit(solution)/shard_map/all_to_all | solution.py:291
  253.1 9.6 %collective-permute-start.19 = (bf16[512,256]{1,0:T(8,128)(2,1)S(1)}, bf16[512,256]{1,0:T(8,128)(2,1)S(1)}, u32[]{:S(2)}, u32[]{:S(2)}) collective-permute-start(bf16[512,256]{1,0:T(8,128)(2,1)S(1)} %copy-done.11), channel_id=1, source_target_pairs={{1,0},{2,1},{3,2},{4,3},{5,4},{6,5},{7,6},{8,7},{9,8},{10,9},{11,1... | collective-permute-start | bytes 786440 | tf_op jit(solution)/shard_map/ppermute | solution.py:45
  263.8 8.3 %second_section.2.refs_0_ = f32[3,512,256]{2,1,0:T(8,128)} custom-call(bf16[4096,256]{1,0:T(8,128)(2,1)} %bitcast.30.coef, bf16[768,4096]{1,0:T(8,128)(2,1)} %turn.1.refs_5_.weights, bf16[512,256]{1,0:T(8,128)(2,1)} %copy-done.9, bf16[512,256]{1,0:T(8,128)(2,1)} %get-tuple-element.8.refs_0_.refs_6_.x1, bf16[512,256]{1,0:T(8,128)(2,1)} %copy-done.10, ...), custom_call_target="tpu_custom_call" | custom-call | flops 1610612736 | bytes 8388608 | tf_op jit(solution)/shard_map/second_section/pallas_call | solution.py:57
  272.1 13.3 %collective-permute-done.18.x0 = bf16[512,256]{1,0:T(8,128)(2,1)S(1)} collective-permute-done((bf16[512,256]{1,0:T(8,128)(2,1)S(1)}, bf16[512,256]{1,0:T(8,128)(2,1)S(1)}, u32[]{:S(2)}, u32[]{:S(2)}) %collective-permute-start.18) | collective-permute-done | bytes 262176 | tf_op jit(solution)/shard_map/ppermute | solution.py:45
  286.2 8.3 %second_section.3 = f32[3,512,256]{2,1,0:T(8,128)} custom-call(bf16[4096,256]{1,0:T(8,128)(2,1)} %bitcast.28.coef, bf16[768,4096]{1,0:T(8,128)(2,1)} %turn.1.refs_5_.weights, bf16[512,256]{1,0:T(8,128)(2,1)} %copy-done.15, bf16[512,256]{1,0:T(8,128)(2,1)} %get-tuple-element.9.refs_0_.x1, ...), custom_call_target="tpu_custom_call", output_to_operand_aliasing={{}: (7, {})} | custom-call | flops 1610612736 | bytes 8388608 | tf_op jit(solution)/shard_map/second_section/pallas_call | solution.py:57
  (123 shorter events, 63.7 us)
Async XLA Ops:
  6.2 54.1 %all-to-all-start = ((bf16[4,4,2,8,32,256]{5,4,3,2,1,0:T(8,128)(2,1)}), bf16[4,4,2,8,32,256]{5,4,3,2,1,0:T(8,128)(2,1)}, u32[]{:S(2)}, u32[]{:S(2)}) async-start(bf16[4,4,2,8,32,256]{5,4,3,2,1,0:T(8,128)(2,1)} %mask.1), calls=%async_computation | async-start | bytes 8388608 | tf_op jit(solution)/shard_map/all_to_all | solution.py:280
  17.0 8.7 %collective-permute-start = (bf16[512,256]{1,0:T(8,128)(2,1)S(1)}, bf16[512,256]{1,0:T(8,128)(2,1)S(1)}, u32[]{:S(2)}, u32[]{:S(2)}) collective-permute-start(bf16[512,256]{1,0:T(8,128)(2,1)S(1)} %pad_maximum_fusion.1.refs_7_.refs_0_.x1), channel_id=1, source_target_pairs={{32,0},{64,32},{96,64},{0,96},{33,1},{65,33},{97,65},{1,97},{34,2}... | collective-permute-start | bytes 786440 | tf_op jit(solution)/shard_map/ppermute | solution.py:49
  17.1 33.5 %collective-permute-start.1 = (bf16[512,256]{1,0:T(8,128)(2,1)S(1)}, bf16[512,256]{1,0:T(8,128)(2,1)S(1)}, u32[]{:S(2)}, u32[]{:S(2)}) collective-permute-start(bf16[512,256]{1,0:T(8,128)(2,1)S(1)} %pad_maximum_fusion.1.refs_7_.refs_0_.x1), channel_id=1, source_target_pairs={{96,0},{0,32},{32,64},{64,96},{97,1},{1,33},{33,65},{65,97},{98,2}... | collective-permute-start | bytes 786440 | tf_op jit(solution)/shard_map/ppermute | solution.py:49
  19.1 31.5 %collective-permute-start.2 = (bf16[512,256]{1,0:T(8,128)(2,1)S(1)}, bf16[512,256]{1,0:T(8,128)(2,1)}, u32[]{:S(2)}, u32[]{:S(2)}) collective-permute-start(bf16[512,256]{1,0:T(8,128)(2,1)S(1)} %pad_maximum_fusion.1.refs_7_.refs_0_.x1), channel_id=1, source_target_pairs={{64,0},{96,32},{0,64},{32,96},{65,1},{97,33},{1,65},{33,97},{66,2}... | collective-permute-start | bytes 786440 | tf_op jit(solution)/shard_map/ppermute | solution.py:49
  23.4 27.3 %collective-permute-start.3 = (bf16[512,256]{1,0:T(8,128)(2,1)S(1)}, bf16[512,256]{1,0:T(8,128)(2,1)S(1)}, u32[]{:S(2)}, u32[]{:S(2)}) collective-permute-start(bf16[512,256]{1,0:T(8,128)(2,1)S(1)} %pad_maximum_fusion.2.refs_0_.x1), channel_id=1, source_target_pairs={{32,0},{64,32},{96,64},{0,96},{33,1},{65,33},{97,65},{1,97},{34,2}... | collective-permute-start | bytes 786440 | tf_op jit(solution)/shard_map/ppermute | solution.py:49
  23.5 27.2 %collective-permute-start.4 = (bf16[512,256]{1,0:T(8,128)(2,1)S(1)}, bf16[512,256]{1,0:T(8,128)(2,1)S(1)}, u32[]{:S(2)}, u32[]{:S(2)}) collective-permute-start(bf16[512,256]{1,0:T(8,128)(2,1)S(1)} %pad_maximum_fusion.2.refs_0_.x1), channel_id=1, source_target_pairs={{96,0},{0,32},{32,64},{64,96},{97,1},{1,33},{33,65},{65,97},{98,2}... | collective-permute-start | bytes 786440 | tf_op jit(solution)/shard_map/ppermute | solution.py:49
  25.7 25.0 %collective-permute-start.5 = (bf16[512,256]{1,0:T(8,128)(2,1)S(1)}, bf16[512,256]{1,0:T(8,128)(2,1)S(1)}, u32[]{:S(2)}, u32[]{:S(2)}) collective-permute-start(bf16[512,256]{1,0:T(8,128)(2,1)S(1)} %pad_maximum_fusion.2.refs_0_.x1), channel_id=1, source_target_pairs={{64,0},{96,32},{0,64},{32,96},{65,1},{97,33},{1,65},{33,97},{66,2}... | collective-permute-start | bytes 786440 | tf_op jit(solution)/shard_map/ppermute | solution.py:49
  65.7 35.4 %all-to-all-start.2 = ((bf16[32,128,256]{2,1,0:T(8,128)(2,1)}), bf16[32,128,256]{2,1,0:T(8,128)(2,1)}, u32[]{:S(2)}, u32[]{:S(2)}) async-start(bf16[32,128,256]{2,1,0:T(8,128)(2,1)} %bitcast.144), calls=%async_computation.2 | async-start | bytes 4194304 | tf_op jit(solution)/shard_map/all_to_all | solution.py:291
  101.1 74.9 %all-to-all-start.1 = ((bf16[32,128,256]{2,1,0:T(8,128)(2,1)}), bf16[32,128,256]{2,1,0:T(8,128)(2,1)}, u32[]{:S(2)}, u32[]{:S(2)}) async-start(bf16[32,128,256]{2,1,0:T(8,128)(2,1)} %bitcast.137), calls=%async_computation.1 | async-start | bytes 4194304 | tf_op jit(solution)/shard_map/all_to_all | solution.py:291
  106.0 31.0 %collective-permute-start.8 = (bf16[512,256]{1,0:T(8,128)(2,1)S(1)}, bf16[512,256]{1,0:T(8,128)(2,1)S(1)}, u32[]{:S(2)}, u32[]{:S(2)}) collective-permute-start(bf16[512,256]{1,0:T(8,128)(2,1)S(1)} %copy-done.5), channel_id=1, source_target_pairs={{0,1},{1,2},{2,3},{3,4},{4,5},{5,6},{6,7},{7,8},{8,9},{9,10},{10,1... | collective-permute-start | bytes 786440 | tf_op jit(solution)/shard_map/ppermute | solution.py:45
  108.0 29.0 %collective-permute-start.9 = (bf16[512,256]{1,0:T(8,128)(2,1)S(1)}, bf16[512,256]{1,0:T(8,128)(2,1)S(1)}, u32[]{:S(2)}, u32[]{:S(2)}) collective-permute-start(bf16[512,256]{1,0:T(8,128)(2,1)S(1)} %copy-done.5), channel_id=1, source_target_pairs={{1,0},{2,1},{3,2},{4,3},{5,4},{6,5},{7,6},{8,7},{9,8},{10,9},{11,1... | collective-permute-start | bytes 786440 | tf_op jit(solution)/shard_map/ppermute | solution.py:45
  149.5 16.3 %collective-permute-start.10 = (bf16[512,256]{1,0:T(8,128)(2,1)}, bf16[512,256]{1,0:T(8,128)(2,1)S(1)}, u32[]{:S(2)}, u32[]{:S(2)}) collective-permute-start(bf16[512,256]{1,0:T(8,128)(2,1)} %get-tuple-element.8.refs_0_.refs_6_.x1), channel_id=1, source_target_pairs={{32,0},{64,32},{96,64},{0,96},{33,1},{65,33},{97,65},{1,97},{34,2}... | collective-permute-start | bytes 786440 | tf_op jit(solution)/shard_map/ppermute | solution.py:49
  149.5 16.3 %collective-permute-start.11 = (bf16[512,256]{1,0:T(8,128)(2,1)}, bf16[512,256]{1,0:T(8,128)(2,1)S(1)}, u32[]{:S(2)}, u32[]{:S(2)}) collective-permute-start(bf16[512,256]{1,0:T(8,128)(2,1)} %get-tuple-element.8.refs_0_.refs_6_.x1), channel_id=1, source_target_pairs={{96,0},{0,32},{32,64},{64,96},{97,1},{1,33},{33,65},{65,97},{98,2}... | collective-permute-start | bytes 786440 | tf_op jit(solution)/shard_map/ppermute | solution.py:49
  151.5 14.3 %collective-permute-start.12 = (bf16[512,256]{1,0:T(8,128)(2,1)}, bf16[512,256]{1,0:T(8,128)(2,1)S(1)}, u32[]{:S(2)}, u32[]{:S(2)}) collective-permute-start(bf16[512,256]{1,0:T(8,128)(2,1)} %get-tuple-element.8.refs_0_.refs_6_.x1), channel_id=1, source_target_pairs={{64,0},{96,32},{0,64},{32,96},{65,1},{97,33},{1,65},{33,97},{66,2}... | collective-permute-start | bytes 786440 | tf_op jit(solution)/shard_map/ppermute | solution.py:49
  156.0 12.1 %collective-permute-start.13 = (bf16[512,256]{1,0:T(8,128)(2,1)}, bf16[512,256]{1,0:T(8,128)(2,1)S(1)}, u32[]{:S(2)}, u32[]{:S(2)}) collective-permute-start(bf16[512,256]{1,0:T(8,128)(2,1)} %get-tuple-element.8.refs_0_.refs_6_.x1), channel_id=1, source_target_pairs={{0,1},{1,2},{2,3},{3,4},{4,5},{5,6},{6,7},{7,8},{8,9},{9,10},{10,1... | collective-permute-start | bytes 786440 | tf_op jit(solution)/shard_map/ppermute | solution.py:45
  157.9 12.1 %collective-permute-start.14 = (bf16[512,256]{1,0:T(8,128)(2,1)}, bf16[512,256]{1,0:T(8,128)(2,1)S(1)}, u32[]{:S(2)}, u32[]{:S(2)}) collective-permute-start(bf16[512,256]{1,0:T(8,128)(2,1)} %get-tuple-element.8.refs_0_.refs_6_.x1), channel_id=1, source_target_pairs={{1,0},{2,1},{3,2},{4,3},{5,4},{6,5},{7,6},{8,7},{9,8},{10,9},{11,1... | collective-permute-start | bytes 786440 | tf_op jit(solution)/shard_map/ppermute | solution.py:45
  176.0 68.7 %all-to-all-start.4 = ((bf16[32,128,256]{2,1,0:T(8,128)(2,1)}), bf16[32,128,256]{2,1,0:T(8,128)(2,1)}, u32[]{:S(2)}, u32[]{:S(2)}) async-start(bf16[32,128,256]{2,1,0:T(8,128)(2,1)} %bitcast.142), calls=%async_computation.4 | async-start | bytes 4194304 | tf_op jit(solution)/shard_map/all_to_all | solution.py:291
  182.0 33.5 %collective-permute-start.6 = (bf16[512,256]{1,0:T(8,128)(2,1)S(1)}, bf16[512,256]{1,0:T(8,128)(2,1)S(1)}, u32[]{:S(2)}, u32[]{:S(2)}) collective-permute-start(bf16[512,256]{1,0:T(8,128)(2,1)S(1)} %copy-done.3), channel_id=1, source_target_pairs={{0,1},{1,2},{2,3},{3,4},{4,5},{5,6},{6,7},{7,8},{8,9},{9,10},{10,1... | collective-permute-start | bytes 786440 | tf_op jit(solution)/shard_map/ppermute | solution.py:45
  184.1 31.4 %collective-permute-start.7 = (bf16[512,256]{1,0:T(8,128)(2,1)S(1)}, bf16[512,256]{1,0:T(8,128)(2,1)S(1)}, u32[]{:S(2)}, u32[]{:S(2)}) collective-permute-start(bf16[512,256]{1,0:T(8,128)(2,1)S(1)} %copy-done.3), channel_id=1, source_target_pairs={{1,0},{2,1},{3,2},{4,3},{5,4},{6,5},{7,6},{8,7},{9,8},{10,9},{11,1... | collective-permute-start | bytes 786440 | tf_op jit(solution)/shard_map/ppermute | solution.py:45
  228.5 7.9 %collective-permute-start.16 = (bf16[512,256]{1,0:T(8,128)(2,1)}, bf16[512,256]{1,0:T(8,128)(2,1)S(1)}, u32[]{:S(2)}, u32[]{:S(2)}) collective-permute-start(bf16[512,256]{1,0:T(8,128)(2,1)} %get-tuple-element.9.refs_0_.x1), channel_id=1, source_target_pairs={{96,0},{0,32},{32,64},{64,96},{97,1},{1,33},{33,65},{65,97},{98,2}... | collective-permute-start | bytes 786440 | tf_op jit(solution)/shard_map/ppermute | solution.py:49
  230.6 8.1 %collective-permute-start.17 = (bf16[512,256]{1,0:T(8,128)(2,1)}, bf16[512,256]{1,0:T(8,128)(2,1)S(1)}, u32[]{:S(2)}, u32[]{:S(2)}) collective-permute-start(bf16[512,256]{1,0:T(8,128)(2,1)} %get-tuple-element.9.refs_0_.x1), channel_id=1, source_target_pairs={{64,0},{96,32},{0,64},{32,96},{65,1},{97,33},{1,65},{33,97},{66,2}... | collective-permute-start | bytes 786440 | tf_op jit(solution)/shard_map/ppermute | solution.py:49
  244.7 40.7 %all-to-all-start.3 = ((bf16[32,128,256]{2,1,0:T(8,128)(2,1)}), bf16[32,128,256]{2,1,0:T(8,128)(2,1)}, u32[]{:S(2)}, u32[]{:S(2)}) async-start(bf16[32,128,256]{2,1,0:T(8,128)(2,1)} %bitcast.143), calls=%async_computation.3 | async-start | bytes 4194304 | tf_op jit(solution)/shard_map/all_to_all | solution.py:291
  251.0 34.4 %collective-permute-start.18 = (bf16[512,256]{1,0:T(8,128)(2,1)S(1)}, bf16[512,256]{1,0:T(8,128)(2,1)S(1)}, u32[]{:S(2)}, u32[]{:S(2)}) collective-permute-start(bf16[512,256]{1,0:T(8,128)(2,1)S(1)} %copy-done.11), channel_id=1, source_target_pairs={{0,1},{1,2},{2,3},{3,4},{4,5},{5,6},{6,7},{7,8},{8,9},{9,10},{10,1... | collective-permute-start | bytes 786440 | tf_op jit(solution)/shard_map/ppermute | solution.py:45
  253.1 32.3 %collective-permute-start.19 = (bf16[512,256]{1,0:T(8,128)(2,1)S(1)}, bf16[512,256]{1,0:T(8,128)(2,1)S(1)}, u32[]{:S(2)}, u32[]{:S(2)}) collective-permute-start(bf16[512,256]{1,0:T(8,128)(2,1)S(1)} %copy-done.11), channel_id=1, source_target_pairs={{1,0},{2,1},{3,2},{4,3},{5,4},{6,5},{7,6},{8,7},{9,8},{10,9},{11,1... | collective-permute-start | bytes 786440 | tf_op jit(solution)/shard_map/ppermute | solution.py:45
  (34 other events, 235.6 us)

commit v4 on v3

--- a/solution.py
+++ b/solution.py
@@ -338,7 +338,7 @@
     begun = [start(part) for part in range(PARTS)]
     around = [gathered(slips) for slips, _ in begun]
     slabs = [neighbours(slips) for slips, _ in begun]
-    before = (left, columns, *around[1])
+    before = (left, columns, *around[1], *[v[k] for v in slabs for k in (0, 2)])
     coefs = [coefficients_of(around[0], planes, right, before)]
     arrived = [sent(coefs[0])]
     coefs.append(coefficients_of(around[1], planes, right, (coefs[0],)))

time: 296 us -> 243 us (0.82)
  waiting for transfers between devices: 103 us -> 54.4 us
    ppermute x8, waiting for transfers between devices: 61.2 us -> 16.5 us  [beside(): return lax.ppermute(slabs, ALL, pairs)]
    ppermute x12, starting transfers between devices: 28.5 us -> 21.8 us  [from_z(): return lax.ppermute(slabs, 'z', [((i + dz) % SIDE, i) for i in range(SIDE)])]
    all_to_all x1, waiting for transfers between devices: 9.65 us -> 3.2 us  [on_device(): right = lax.all_to_all(right, 'y', split_axis=0, concat_axis=0, tiled=True)]
    all_to_all x4, starting transfers between devices: 22.5 us -> 26.9 us  [sent(): lax.all_to_all(coef, ('y', 'x', 'core'), split_axis=0, concat_axis=0, til...]
    ppermute x12, waiting for transfers between devices: 7.09 us -> 10.1 us  [from_z(): return lax.ppermute(slabs, 'z', [((i + dz) % SIDE, i) for i in range(SIDE)])]
    unnamed x71 -> x65, local copies, waits for them, and re-layouts: 6.33 us -> 4.29 us
  transfers between devices with their start and end apart: 25 -> 25, of which waited for: 11 -> 9; matrix products, arithmetic and copies ran while one was open for 3% -> 3% of each run, Pallas kernels for 21% -> 25%
where the time goes in v4:
time: 243 us; the launch traced here: 242 us
  starting transfers between devices  95.6 us (39%)
  Pallas kernels  79.2 us (33%)
  waiting for transfers between devices  54.4 us (22%)
  local copies, waits for them, and re-layouts  6.62 us (3%)
  other arithmetic  4.6 us (2%)
    pallas_call x12, Pallas kernels, call(): pl.pallas_call(kernel, grid=grid, in_specs=in_specs, out_specs=out_specs,...  79.2 us
    ppermute x8, starting transfers between devices, beside(): return lax.ppermute(slabs, ALL, pairs)  41.9 us
    all_to_all x4, starting transfers between devices, sent(): lax.all_to_all(coef, ('y', 'x', 'core'), split_axis=0, concat_axis=0, til...  26.9 us
    all_to_all x4, waiting for transfers between devices, sent(): lax.all_to_all(coef, ('y', 'x', 'core'), split_axis=0, concat_axis=0, til...  24.7 us
    ppermute x12, starting transfers between devices, from_z(): return lax.ppermute(slabs, 'z', [((i + dz) % SIDE, i) for i in range(SIDE)])  21.8 us
    ppermute x8, waiting for transfers between devices, beside(): return lax.ppermute(slabs, ALL, pairs)  16.5 us
    ppermute x12, waiting for transfers between devices, from_z(): return lax.ppermute(slabs, 'z', [((i + dz) % SIDE, i) for i in range(SIDE)])  10.1 us
    all_to_all x1, starting transfers between devices, on_device(): right = lax.all_to_all(right, 'y', split_axis=0, concat_axis=0, tiled=True)  4.98 us
  transfers between devices with their start and end apart: 25, of which 9 were waited for; matrix products, arithmetic and copies ran while one was open for 3% of the time, Pallas kernels for 25%

profile of v4, /device:TPU:32, one launch (start us, length us, event | category | flops | bytes accessed | tf_op | source)
XLA Modules:
  0.0 241.7 jit_solution(4629941859376697016)
XLA Ops:
  1.3 4.9 %mask.1 = bf16[4,4,2,8,32,256]{5,4,3,2,1,0:T(8,128)(2,1)} custom-call(s32[2]{0:T(128)} %pad_add_fusion.1.place, s32[8,16]{1,0:T(8,128)} %ranks.1, bf16[8,4,4,2,32,256]{5,4,3,2,1,0:T(8,128)(2,1)} %bitcast.154), custom_call_target="tpu_custom_call" | custom-call | bytes 8388608 | tf_op jit(solution)/shard_map/mask/pallas_call | solution.py:57
  6.1 5.0 %all-to-all-start = ((bf16[4,4,2,8,32,256]{5,4,3,2,1,0:T(8,128)(2,1)}), bf16[4,4,2,8,32,256]{5,4,3,2,1,0:T(8,128)(2,1)}, u32[]{:S(2)}, u32[]{:S(2)}) async-start(bf16[4,4,2,8,32,256]{5,4,3,2,1,0:T(8,128)(2,1)} %mask.1), calls=%async_computation | async-start | bytes 8388608 | tf_op jit(solution)/shard_map/all_to_all | solution.py:280
  19.0 4.2 %collective-permute-start.2 = (bf16[512,256]{1,0:T(8,128)(2,1)S(1)}, bf16[512,256]{1,0:T(8,128)(2,1)S(1)}, u32[]{:S(2)}, u32[]{:S(2)}) collective-permute-start(bf16[512,256]{1,0:T(8,128)(2,1)S(1)} %pad_maximum_fusion.1.refs_7_.refs_0_.x1), channel_id=1, source_target_pairs={{64,0},{96,32},{0,64},{32,96},{65,1},{97,33},{1,65},{33,97},{66,2}... | collective-permute-start | bytes 786440 | tf_op jit(solution)/shard_map/ppermute | solution.py:49
  25.1 7.9 %collective-permute-start.9 = (bf16[512,256]{1,0:T(8,128)(2,1)S(1)}, bf16[512,256]{1,0:T(8,128)(2,1)S(1)}, u32[]{:S(2)}, u32[]{:S(2)}) collective-permute-start(bf16[512,256]{1,0:T(8,128)(2,1)S(1)} %pad_maximum_fusion.1.refs_7_.refs_0_.x1), channel_id=1, source_target_pairs={{1,0},{2,1},{3,2},{4,3},{5,4},{6,5},{7,6},{8,7},{9,8},{10,9},{11,1... | collective-permute-start | bytes 786440 | tf_op jit(solution)/shard_map/ppermute | solution.py:45
  35.0 7.9 %collective-permute-start.7 = (bf16[512,256]{1,0:T(8,128)(2,1)S(1)}, bf16[512,256]{1,0:T(8,128)(2,1)S(1)}, u32[]{:S(2)}, u32[]{:S(2)}) collective-permute-start(bf16[512,256]{1,0:T(8,128)(2,1)S(1)} %pad_maximum_fusion.2.refs_0_.x1), channel_id=1, source_target_pairs={{1,0},{2,1},{3,2},{4,3},{5,4},{6,5},{7,6},{8,7},{9,8},{10,9},{11,1... | collective-permute-start | bytes 786440 | tf_op jit(solution)/shard_map/ppermute | solution.py:45
  48.1 13.1 %turn.1.refs_5_.weights = bf16[768,4096]{1,0:T(8,128)(2,1)} custom-call(bf16[8,4,4,3,32,256]{5,4,3,2,1,0:T(8,128)(2,1)} %bitcast.153), custom_call_target="tpu_custom_call" | custom-call | bytes 8388608 | tf_op jit(solution)/shard_map/turn/pallas_call | solution.py:57
  65.9 5.3 %coefficients.4.refs_5_ = bf16[32,4,32,256]{3,2,1,0:T(8,128)(2,1)} custom-call(s32[4]{0:T(128)} %pad_add_fusion.planes, bf16[512,256]{1,0:T(8,128)(2,1)} %copy-done.3, bf16[512,256]{1,0:T(8,128)(2,1)} %copy-done.15, bf16[512,256]{1,0:T(8,128)(2,1)} %collective-permute-done.4.refs_2_, bf16[512,256]{1,0:T(8,128)(2,1)} %collective-permute-done.5.refs_3_, ...), custom_call_target="tpu_custom_call" | custom-call | flops 1073741824 | bytes 8388608 | tf_op jit(solution)/shard_map/coefficients/pallas_call | solution.py:57
  71.2 7.9 %all-to-all-start.2 = ((bf16[32,128,256]{2,1,0:T(8,128)(2,1)}), bf16[32,128,256]{2,1,0:T(8,128)(2,1)}, u32[]{:S(2)}, u32[]{:S(2)}) async-start(bf16[32,128,256]{2,1,0:T(8,128)(2,1)} %bitcast.142), calls=%async_computation.2 | async-start | bytes 4194304 | tf_op jit(solution)/shard_map/all_to_all | solution.py:291
  79.1 5.3 %coefficients.5.refs_0_ = bf16[32,4,32,256]{3,2,1,0:T(8,128)(2,1)} custom-call(s32[4]{0:T(128)} %pad_add_fusion.planes, bf16[512,256]{1,0:T(8,128)(2,1)} %copy-done.2, bf16[512,256]{1,0:T(8,128)(2,1)} %copy-done.7, bf16[512,256]{1,0:T(8,128)(2,1)} %copy-done.8, bf16[512,256]{1,0:T(8,128)(2,1)} %copy-done.9, ...), custom_call_target="tpu_custom_call" | custom-call | flops 1073741824 | bytes 8388608 | tf_op jit(solution)/shard_map/coefficients/pallas_call | solution.py:57
  84.4 24.6 %all-to-all-done.2 = bf16[32,128,256]{2,1,0:T(8,128)(2,1)} async-done(((bf16[32,128,256]{2,1,0:T(8,128)(2,1)}), bf16[32,128,256]{2,1,0:T(8,128)(2,1)}, u32[]{:S(2)}, u32[]{:S(2)}) %all-to-all-start.2) | async-done | bytes 2097184 | tf_op jit(solution)/shard_map/all_to_all | solution.py:291
  109.1 4.8 %all-to-all-start.1 = ((bf16[32,128,256]{2,1,0:T(8,128)(2,1)}), bf16[32,128,256]{2,1,0:T(8,128)(2,1)}, u32[]{:S(2)}, u32[]{:S(2)}) async-start(bf16[32,128,256]{2,1,0:T(8,128)(2,1)} %bitcast.137), calls=%async_computation.1 | async-start | bytes 4194304 | tf_op jit(solution)/shard_map/all_to_all | solution.py:291
  113.8 4.1 %near.3 = f32[768,256]{1,0:T(8,128)} custom-call(bf16[512,256]{1,0:T(8,128)(2,1)} %copy-done.10, bf16[512,256]{1,0:T(8,128)(2,1)} %copy-done.3, bf16[512,256]{1,0:T(8,128)(2,1)} %copy-done.11, bf16[3,3,2,256,256]{4,3,2,1,0:T(8,128)(2,1)} %bitcast.138, bf16[32,4,32,256]{3,2,1,0:T(8,128)(2,1)} %coefficients.5.refs_0_), custom_call_target="tpu_custom_call" | custom-call | flops 603979776 | bytes 8388608 | tf_op jit(solution)/shard_map/near/pallas_call | solution.py:57
  117.9 7.6 %first_section.2 = (bf16[512,256]{1,0:T(8,128)(2,1)}, f32[3,256,256]{2,1,0:T(8,128)}, f32[256,256]{1,0:T(8,128)}) custom-call(bf16[4096,256]{1,0:T(8,128)(2,1)} %bitcast.26.coef, bf16[768,4096]{1,0:T(8,128)(2,1)} %turn.1.refs_5_.weights, f32[768,256]{1,0:T(8,128)} %near.3, f32[3,256,256]{2,1,0:T(8,128)} %bitcast.152, ...), custom_call_target="tpu_custom_call" | custom-call | flops 1610612736 | bytes 8388608 | tf_op jit(solution)/shard_map/first_section/pallas_call | solution.py:57
  131.8 7.9 %collective-permute-start.14 = (bf16[512,256]{1,0:T(8,128)(2,1)}, bf16[512,256]{1,0:T(8,128)(2,1)S(1)}, u32[]{:S(2)}, u32[]{:S(2)}) collective-permute-start(bf16[512,256]{1,0:T(8,128)(2,1)} %get-tuple-element.8.refs_0_.refs_6_.x1), channel_id=1, source_target_pairs={{1,0},{2,1},{3,2},{4,3},{5,4},{6,5},{7,6},{8,7},{9,8},{10,9},{11,1... | collective-permute-start | bytes 786440 | tf_op jit(solution)/shard_map/ppermute | solution.py:45
  144.8 5.3 %coefficients.6.refs_0_ = bf16[32,4,32,256]{3,2,1,0:T(8,128)(2,1)} custom-call(s32[4]{0:T(128)} %pad_add_fusion.planes, bf16[512,256]{1,0:T(8,128)(2,1)} %get-tuple-element.8.refs_0_.refs_6_.x1, bf16[512,256]{1,0:T(8,128)(2,1)} %copy-done.18, bf16[512,256]{1,0:T(8,128)(2,1)} %copy-done.19, bf16[512,256]{1,0:T(8,128)(2,1)} %copy-done.20, ...), custom_call_target="tpu_custom_call" | custom-call | flops 1073741824 | bytes 8388608 | tf_op jit(solution)/shard_map/coefficients/pallas_call | solution.py:57
  150.1 6.6 %all-to-all-start.4 = ((bf16[32,128,256]{2,1,0:T(8,128)(2,1)}), bf16[32,128,256]{2,1,0:T(8,128)(2,1)}, u32[]{:S(2)}, u32[]{:S(2)}) async-start(bf16[32,128,256]{2,1,0:T(8,128)(2,1)} %bitcast.143), calls=%async_computation.4 | async-start | bytes 4194304 | tf_op jit(solution)/shard_map/all_to_all | solution.py:291
  156.8 4.1 %near.2 = f32[768,256]{1,0:T(8,128)} custom-call(bf16[512,256]{1,0:T(8,128)(2,1)} %copy-done.5, bf16[512,256]{1,0:T(8,128)(2,1)} %copy-done.2, bf16[512,256]{1,0:T(8,128)(2,1)} %copy-done.6, bf16[3,3,2,256,256]{4,3,2,1,0:T(8,128)(2,1)} %bitcast.139, bf16[32,4,32,256]{3,2,1,0:T(8,128)(2,1)} %coefficients.5.refs_0_), custom_call_target="tpu_custom_call" | custom-call | flops 603979776 | bytes 8388608 | tf_op jit(solution)/shard_map/near/pallas_call | solution.py:57
  160.8 7.6 %first_section.3 = (bf16[512,256]{1,0:T(8,128)(2,1)}, f32[3,256,256]{2,1,0:T(8,128)}, f32[256,256]{1,0:T(8,128)}) custom-call(bf16[4096,256]{1,0:T(8,128)(2,1)} %bitcast.23.coef, bf16[768,4096]{1,0:T(8,128)(2,1)} %turn.1.refs_5_.weights, f32[768,256]{1,0:T(8,128)} %near.2, f32[3,256,256]{2,1,0:T(8,128)} %bitcast.148, ...), custom_call_target="tpu_custom_call" | custom-call | flops 1610612736 | bytes 8388608 | tf_op jit(solution)/shard_map/first_section/pallas_call | solution.py:57
  184.2 5.3 %coefficients.7.refs_0_ = bf16[32,4,32,256]{3,2,1,0:T(8,128)(2,1)} custom-call(s32[4]{0:T(128)} %pad_add_fusion.planes, bf16[512,256]{1,0:T(8,128)(2,1)} %get-tuple-element.9.refs_0_.x1, bf16[512,256]{1,0:T(8,128)(2,1)} %copy-done.23, bf16[512,256]{1,0:T(8,128)(2,1)} %copy-done.24, bf16[512,256]{1,0:T(8,128)(2,1)} %copy-done.25, ...), custom_call_target="tpu_custom_call" | custom-call | flops 1073741824 | bytes 8388608 | tf_op jit(solution)/shard_map/coefficients/pallas_call | solution.py:57
  189.6 7.6 %all-to-all-start.3 = ((bf16[32,128,256]{2,1,0:T(8,128)(2,1)}), bf16[32,128,256]{2,1,0:T(8,128)(2,1)}, u32[]{:S(2)}, u32[]{:S(2)}) async-start(bf16[32,128,256]{2,1,0:T(8,128)(2,1)} %bitcast.144), calls=%async_computation.3 | async-start | bytes 4194304 | tf_op jit(solution)/shard_map/all_to_all | solution.py:291
  199.4 10.5 %collective-permute-start.19 = (bf16[512,256]{1,0:T(8,128)(2,1)S(1)}, bf16[512,256]{1,0:T(8,128)(2,1)S(1)}, u32[]{:S(2)}, u32[]{:S(2)}) collective-permute-start(bf16[512,256]{1,0:T(8,128)(2,1)S(1)} %copy-done.14), channel_id=1, source_target_pairs={{1,0},{2,1},{3,2},{4,3},{5,4},{6,5},{7,6},{8,7},{9,8},{10,9},{11,1... | collective-permute-start | bytes 786440 | tf_op jit(solution)/shard_map/ppermute | solution.py:45
  211.0 8.3 %second_section.2.refs_0_ = f32[3,512,256]{2,1,0:T(8,128)} custom-call(bf16[4096,256]{1,0:T(8,128)(2,1)} %bitcast.30.coef, bf16[768,4096]{1,0:T(8,128)(2,1)} %turn.1.refs_5_.weights, bf16[512,256]{1,0:T(8,128)(2,1)} %copy-done.12, bf16[512,256]{1,0:T(8,128)(2,1)} %get-tuple-element.8.refs_0_.refs_6_.x1, bf16[512,256]{1,0:T(8,128)(2,1)} %copy-done.13, ...), custom_call_target="tpu_custom_call" | custom-call | flops 1610612736 | bytes 8388608 | tf_op jit(solution)/shard_map/second_section/pallas_call | solution.py:57
  219.2 13.4 %collective-permute-done.18.x0 = bf16[512,256]{1,0:T(8,128)(2,1)S(1)} collective-permute-done((bf16[512,256]{1,0:T(8,128)(2,1)S(1)}, bf16[512,256]{1,0:T(8,128)(2,1)S(1)}, u32[]{:S(2)}, u32[]{:S(2)}) %collective-permute-start.18) | collective-permute-done | bytes 262176 | tf_op jit(solution)/shard_map/ppermute | solution.py:45
  233.4 8.3 %second_section.3 = f32[3,512,256]{2,1,0:T(8,128)} custom-call(bf16[4096,256]{1,0:T(8,128)(2,1)} %bitcast.28.coef, bf16[768,4096]{1,0:T(8,128)(2,1)} %turn.1.refs_5_.weights, bf16[512,256]{1,0:T(8,128)(2,1)} %copy-done.16, bf16[512,256]{1,0:T(8,128)(2,1)} %get-tuple-element.9.refs_0_.x1, ...), custom_call_target="tpu_custom_call", output_to_operand_aliasing={{}: (7, {})} | custom-call | flops 1610612736 | bytes 8388608 | tf_op jit(solution)/shard_map/second_section/pallas_call | solution.py:57
  (117 shorter events, 53.1 us)
Async XLA Ops:
  6.1 59.7 %all-to-all-start = ((bf16[4,4,2,8,32,256]{5,4,3,2,1,0:T(8,128)(2,1)}), bf16[4,4,2,8,32,256]{5,4,3,2,1,0:T(8,128)(2,1)}, u32[]{:S(2)}, u32[]{:S(2)}) async-start(bf16[4,4,2,8,32,256]{5,4,3,2,1,0:T(8,128)(2,1)} %mask.1), calls=%async_computation | async-start | bytes 8388608 | tf_op jit(solution)/shard_map/all_to_all | solution.py:280
  16.9 16.2 %collective-permute-start = (bf16[512,256]{1,0:T(8,128)(2,1)S(1)}, bf16[512,256]{1,0:T(8,128)(2,1)S(1)}, u32[]{:S(2)}, u32[]{:S(2)}) collective-permute-start(bf16[512,256]{1,0:T(8,128)(2,1)S(1)} %pad_maximum_fusion.1.refs_7_.refs_0_.x1), channel_id=1, source_target_pairs={{32,0},{64,32},{96,64},{0,96},{33,1},{65,33},{97,65},{1,97},{34,2}... | collective-permute-start | bytes 786440 | tf_op jit(solution)/shard_map/ppermute | solution.py:49
  17.0 18.0 %collective-permute-start.1 = (bf16[512,256]{1,0:T(8,128)(2,1)S(1)}, bf16[512,256]{1,0:T(8,128)(2,1)S(1)}, u32[]{:S(2)}, u32[]{:S(2)}) collective-permute-start(bf16[512,256]{1,0:T(8,128)(2,1)S(1)} %pad_maximum_fusion.1.refs_7_.refs_0_.x1), channel_id=1, source_target_pairs={{96,0},{0,32},{32,64},{64,96},{97,1},{1,33},{33,65},{65,97},{98,2}... | collective-permute-start | bytes 786440 | tf_op jit(solution)/shard_map/ppermute | solution.py:49
  19.0 23.9 %collective-permute-start.2 = (bf16[512,256]{1,0:T(8,128)(2,1)S(1)}, bf16[512,256]{1,0:T(8,128)(2,1)S(1)}, u32[]{:S(2)}, u32[]{:S(2)}) collective-permute-start(bf16[512,256]{1,0:T(8,128)(2,1)S(1)} %pad_maximum_fusion.1.refs_7_.refs_0_.x1), channel_id=1, source_target_pairs={{64,0},{96,32},{0,64},{32,96},{65,1},{97,33},{1,65},{33,97},{66,2}... | collective-permute-start | bytes 786440 | tf_op jit(solution)/shard_map/ppermute | solution.py:49
  23.2 19.8 %collective-permute-start.8 = (bf16[512,256]{1,0:T(8,128)(2,1)S(1)}, bf16[512,256]{1,0:T(8,128)(2,1)S(1)}, u32[]{:S(2)}, u32[]{:S(2)}) collective-permute-start(bf16[512,256]{1,0:T(8,128)(2,1)S(1)} %pad_maximum_fusion.1.refs_7_.refs_0_.x1), channel_id=1, source_target_pairs={{0,1},{1,2},{2,3},{3,4},{4,5},{5,6},{6,7},{7,8},{8,9},{9,10},{10,1... | collective-permute-start | bytes 786440 | tf_op jit(solution)/shard_map/ppermute | solution.py:45
  25.1 19.9 %collective-permute-start.9 = (bf16[512,256]{1,0:T(8,128)(2,1)S(1)}, bf16[512,256]{1,0:T(8,128)(2,1)S(1)}, u32[]{:S(2)}, u32[]{:S(2)}) collective-permute-start(bf16[512,256]{1,0:T(8,128)(2,1)S(1)} %pad_maximum_fusion.1.refs_7_.refs_0_.x1), channel_id=1, source_target_pairs={{1,0},{2,1},{3,2},{4,3},{5,4},{6,5},{7,6},{8,7},{9,8},{10,9},{11,1... | collective-permute-start | bytes 786440 | tf_op jit(solution)/shard_map/ppermute | solution.py:45
  33.1 29.5 %collective-permute-start.6 = (bf16[512,256]{1,0:T(8,128)(2,1)S(1)}, bf16[512,256]{1,0:T(8,128)(2,1)S(1)}, u32[]{:S(2)}, u32[]{:S(2)}) collective-permute-start(bf16[512,256]{1,0:T(8,128)(2,1)S(1)} %pad_maximum_fusion.2.refs_0_.x1), channel_id=1, source_target_pairs={{0,1},{1,2},{2,3},{3,4},{4,5},{5,6},{6,7},{7,8},{8,9},{9,10},{10,1... | collective-permute-start | bytes 786440 | tf_op jit(solution)/shard_map/ppermute | solution.py:45
  35.0 27.6 %collective-permute-start.7 = (bf16[512,256]{1,0:T(8,128)(2,1)S(1)}, bf16[512,256]{1,0:T(8,128)(2,1)S(1)}, u32[]{:S(2)}, u32[]{:S(2)}) collective-permute-start(bf16[512,256]{1,0:T(8,128)(2,1)S(1)} %pad_maximum_fusion.2.refs_0_.x1), channel_id=1, source_target_pairs={{1,0},{2,1},{3,2},{4,3},{5,4},{6,5},{7,6},{8,7},{9,8},{10,9},{11,1... | collective-permute-start | bytes 786440 | tf_op jit(solution)/shard_map/ppermute | solution.py:45
  42.9 19.7 %collective-permute-start.3 = (bf16[512,256]{1,0:T(8,128)(2,1)S(1)}, bf16[512,256]{1,0:T(8,128)(2,1)S(1)}, u32[]{:S(2)}, u32[]{:S(2)}) collective-permute-start(bf16[512,256]{1,0:T(8,128)(2,1)S(1)} %pad_maximum_fusion.2.refs_0_.x1), channel_id=1, source_target_pairs={{32,0},{64,32},{96,64},{0,96},{33,1},{65,33},{97,65},{1,97},{34,2}... | collective-permute-start | bytes 786440 | tf_op jit(solution)/shard_map/ppermute | solution.py:49
  43.0 19.6 %collective-permute-start.4 = (bf16[512,256]{1,0:T(8,128)(2,1)S(1)}, bf16[512,256]{1,0:T(8,128)(2,1)}, u32[]{:S(2)}, u32[]{:S(2)}) collective-permute-start(bf16[512,256]{1,0:T(8,128)(2,1)S(1)} %pad_maximum_fusion.2.refs_0_.x1), channel_id=1, source_target_pairs={{96,0},{0,32},{32,64},{64,96},{97,1},{1,33},{33,65},{65,97},{98,2}... | collective-permute-start | bytes 786440 | tf_op jit(solution)/shard_map/ppermute | solution.py:49
  45.0 17.6 %collective-permute-start.5 = (bf16[512,256]{1,0:T(8,128)(2,1)S(1)}, bf16[512,256]{1,0:T(8,128)(2,1)}, u32[]{:S(2)}, u32[]{:S(2)}) collective-permute-start(bf16[512,256]{1,0:T(8,128)(2,1)S(1)} %pad_maximum_fusion.2.refs_0_.x1), channel_id=1, source_target_pairs={{64,0},{96,32},{0,64},{32,96},{65,1},{97,33},{1,65},{33,97},{66,2}... | collective-permute-start | bytes 786440 | tf_op jit(solution)/shard_map/ppermute | solution.py:49
  71.2 37.8 %all-to-all-start.2 = ((bf16[32,128,256]{2,1,0:T(8,128)(2,1)}), bf16[32,128,256]{2,1,0:T(8,128)(2,1)}, u32[]{:S(2)}, u32[]{:S(2)}) async-start(bf16[32,128,256]{2,1,0:T(8,128)(2,1)} %bitcast.142), calls=%async_computation.2 | async-start | bytes 4194304 | tf_op jit(solution)/shard_map/all_to_all | solution.py:291
  109.1 41.0 %all-to-all-start.1 = ((bf16[32,128,256]{2,1,0:T(8,128)(2,1)}), bf16[32,128,256]{2,1,0:T(8,128)(2,1)}, u32[]{:S(2)}, u32[]{:S(2)}) async-start(bf16[32,128,256]{2,1,0:T(8,128)(2,1)} %bitcast.137), calls=%async_computation.1 | async-start | bytes 4194304 | tf_op jit(solution)/shard_map/all_to_all | solution.py:291
  125.5 14.2 %collective-permute-start.10 = (bf16[512,256]{1,0:T(8,128)(2,1)}, bf16[512,256]{1,0:T(8,128)(2,1)S(1)}, u32[]{:S(2)}, u32[]{:S(2)}) collective-permute-start(bf16[512,256]{1,0:T(8,128)(2,1)} %get-tuple-element.8.refs_0_.refs_6_.x1), channel_id=1, source_target_pairs={{32,0},{64,32},{96,64},{0,96},{33,1},{65,33},{97,65},{1,97},{34,2}... | collective-permute-start | bytes 786440 | tf_op jit(solution)/shard_map/ppermute | solution.py:49
  125.5 14.2 %collective-permute-start.11 = (bf16[512,256]{1,0:T(8,128)(2,1)}, bf16[512,256]{1,0:T(8,128)(2,1)S(1)}, u32[]{:S(2)}, u32[]{:S(2)}) collective-permute-start(bf16[512,256]{1,0:T(8,128)(2,1)} %get-tuple-element.8.refs_0_.refs_6_.x1), channel_id=1, source_target_pairs={{96,0},{0,32},{32,64},{64,96},{97,1},{1,33},{33,65},{65,97},{98,2}... | collective-permute-start | bytes 786440 | tf_op jit(solution)/shard_map/ppermute | solution.py:49
  127.6 13.2 %collective-permute-start.12 = (bf16[512,256]{1,0:T(8,128)(2,1)}, bf16[512,256]{1,0:T(8,128)(2,1)S(1)}, u32[]{:S(2)}, u32[]{:S(2)}) collective-permute-start(bf16[512,256]{1,0:T(8,128)(2,1)} %get-tuple-element.8.refs_0_.refs_6_.x1), channel_id=1, source_target_pairs={{64,0},{96,32},{0,64},{32,96},{65,1},{97,33},{1,65},{33,97},{66,2}... | collective-permute-start | bytes 786440 | tf_op jit(solution)/shard_map/ppermute | solution.py:49
  129.9 13.4 %collective-permute-start.13 = (bf16[512,256]{1,0:T(8,128)(2,1)}, bf16[512,256]{1,0:T(8,128)(2,1)S(1)}, u32[]{:S(2)}, u32[]{:S(2)}) collective-permute-start(bf16[512,256]{1,0:T(8,128)(2,1)} %get-tuple-element.8.refs_0_.refs_6_.x1), channel_id=1, source_target_pairs={{0,1},{1,2},{2,3},{3,4},{4,5},{5,6},{6,7},{7,8},{8,9},{9,10},{10,1... | collective-permute-start | bytes 786440 | tf_op jit(solution)/shard_map/ppermute | solution.py:45
  131.8 12.1 %collective-permute-start.14 = (bf16[512,256]{1,0:T(8,128)(2,1)}, bf16[512,256]{1,0:T(8,128)(2,1)S(1)}, u32[]{:S(2)}, u32[]{:S(2)}) collective-permute-start(bf16[512,256]{1,0:T(8,128)(2,1)} %get-tuple-element.8.refs_0_.refs_6_.x1), channel_id=1, source_target_pairs={{1,0},{2,1},{3,2},{4,3},{5,4},{6,5},{7,6},{8,7},{9,8},{10,9},{11,1... | collective-permute-start | bytes 786440 | tf_op jit(solution)/shard_map/ppermute | solution.py:45
  150.1 39.4 %all-to-all-start.4 = ((bf16[32,128,256]{2,1,0:T(8,128)(2,1)}), bf16[32,128,256]{2,1,0:T(8,128)(2,1)}, u32[]{:S(2)}, u32[]{:S(2)}) async-start(bf16[32,128,256]{2,1,0:T(8,128)(2,1)} %bitcast.143), calls=%async_computation.4 | async-start | bytes 4194304 | tf_op jit(solution)/shard_map/all_to_all | solution.py:291
  170.2 9.6 %collective-permute-start.16 = (bf16[512,256]{1,0:T(8,128)(2,1)}, bf16[512,256]{1,0:T(8,128)(2,1)S(1)}, u32[]{:S(2)}, u32[]{:S(2)}) collective-permute-start(bf16[512,256]{1,0:T(8,128)(2,1)} %get-tuple-element.9.refs_0_.x1), channel_id=1, source_target_pairs={{96,0},{0,32},{32,64},{64,96},{97,1},{1,33},{33,65},{65,97},{98,2}... | collective-permute-start | bytes 786440 | tf_op jit(solution)/shard_map/ppermute | solution.py:49
  170.4 13.1 %collective-permute-start.17 = (bf16[512,256]{1,0:T(8,128)(2,1)}, bf16[512,256]{1,0:T(8,128)(2,1)S(1)}, u32[]{:S(2)}, u32[]{:S(2)}) collective-permute-start(bf16[512,256]{1,0:T(8,128)(2,1)} %get-tuple-element.9.refs_0_.x1), channel_id=1, source_target_pairs={{64,0},{96,32},{0,64},{32,96},{65,1},{97,33},{1,65},{33,97},{66,2}... | collective-permute-start | bytes 786440 | tf_op jit(solution)/shard_map/ppermute | solution.py:49
  189.6 43.0 %all-to-all-start.3 = ((bf16[32,128,256]{2,1,0:T(8,128)(2,1)}), bf16[32,128,256]{2,1,0:T(8,128)(2,1)}, u32[]{:S(2)}, u32[]{:S(2)}) async-start(bf16[32,128,256]{2,1,0:T(8,128)(2,1)} %bitcast.144), calls=%async_computation.3 | async-start | bytes 4194304 | tf_op jit(solution)/shard_map/all_to_all | solution.py:291
  197.3 35.3 %collective-permute-start.18 = (bf16[512,256]{1,0:T(8,128)(2,1)S(1)}, bf16[512,256]{1,0:T(8,128)(2,1)S(1)}, u32[]{:S(2)}, u32[]{:S(2)}) collective-permute-start(bf16[512,256]{1,0:T(8,128)(2,1)S(1)} %copy-done.14), channel_id=1, source_target_pairs={{0,1},{1,2},{2,3},{3,4},{4,5},{5,6},{6,7},{7,8},{8,9},{9,10},{10,1... | collective-permute-start | bytes 786440 | tf_op jit(solution)/shard_map/ppermute | solution.py:45
  199.4 33.2 %collective-permute-start.19 = (bf16[512,256]{1,0:T(8,128)(2,1)S(1)}, bf16[512,256]{1,0:T(8,128)(2,1)S(1)}, u32[]{:S(2)}, u32[]{:S(2)}) collective-permute-start(bf16[512,256]{1,0:T(8,128)(2,1)S(1)} %copy-done.14), channel_id=1, source_target_pairs={{1,0},{2,1},{3,2},{4,3},{5,4},{6,5},{7,6},{8,7},{9,8},{10,9},{11,1... | collective-permute-start | bytes 786440 | tf_op jit(solution)/shard_map/ppermute | solution.py:45
  (31 other events, 262.0 us)
